TPU v7x, 512 devices: a whole 4x8x8 slice. The times are simulated.
512 devices in a mesh: gx: 32 (over y, z_lo, core), gy: 16 (over z_hi, x).
Axes of the slice: x: 4, y: 8, z: 8 (z_hi: 4, z_lo: 2; z = z_hi * 2 + z_lo), core: 2. Of those that a mesh axis runs over, the one named last changes fastest.
Arguments:
- density: float32 [128, 256, 256], P('gx', 'gy'), may hold values from 0.05 to 1
- modes: bfloat16 [12, 128, 256, 256], P(None, 'gx', 'gy'), may hold values from -12 to 12
Outputs:
- sensitivity: float32 [4, 128, 256, 256], P(None, 'gx', 'gy')
All inputs are finite; a program needn't handle non-finite values.
Results may differ from a plain program's by a relative error of at most 0.0014.
Values may be sent and summed in bfloat16 or wider, within the bound.
A program may use at most 64 MiB of HBM per device.

v0:
```python
import jax
import jax.numpy as jnp
import numpy as np
from jax import lax
from jax.sharding import PartitionSpec as P

RADIUS = 3


BETA_SHARP = 16.0
ETA_MID = 0.5
YOUNG_MIN = 0.001
PENALTY = 3.0


def padded_2(cells, sides, width):
    for axis, dim in sides:
        count = lax.axis_size(axis)
        ends = count - 1
        head = lax.slice_in_dim(cells, 0, width, axis=dim)
        tail = lax.slice_in_dim(cells, cells.shape[dim] - width, cells.shape[dim], axis=dim)
        cells = jnp.concatenate(
            [
                lax.ppermute(tail, axis, [(i, (i + 1) % count) for i in range(ends)]),
                cells,
                lax.ppermute(head, axis, [((i + 1) % count, i) for i in range(ends)]),
            ],
            axis=dim,
        )
    return cells


def passed_along(block, axis, distance):
    devices = range(lax.axis_size(axis))
    route = [(i - distance, i) for i in devices if i - distance in devices]
    return lax.ppermute(block, axis, route)


def shortened(x):
    return jax.tree.map(lambda a: a.astype(jnp.bfloat16) if a.dtype == jnp.float32 else a, x)


def element_tables():
    gauss_point = 1.0 / np.sqrt(3.0)
    poisson = 0.3
    lame_first = poisson / ((1.0 + poisson) * (1.0 - 2.0 * poisson))
    lame_shear = 1.0 / (2.0 * (1.0 + poisson))
    elastic = np.zeros((6, 6))
    elastic[:3, :3] = lame_first
    for i in range(3):
        elastic[i, i] += 2.0 * lame_shear
        elastic[3 + i, 3 + i] = lame_shear
    stiffness = np.zeros((24, 24))
    mass_table = np.zeros((24, 24))
    corners = []
    for a in (0, 1):
        for b in (0, 1):
            for d in (0, 1):
                corners.append((2.0 * a - 1.0, 2.0 * b - 1.0, 2.0 * d - 1.0))
    for xi in (-gauss_point, gauss_point):
        for eta in (-gauss_point, gauss_point):
            for zeta in (-gauss_point, gauss_point):
                strain = np.zeros((6, 24))
                shape_rows = np.zeros((3, 24))
                for q in range(8):
                    cx, cy, cz = corners[q]
                    value = (1 + cx * xi) * (1 + cy * eta) * (1 + cz * zeta) / 8.0
                    grad_x = 2.0 * cx * (1 + cy * eta) * (1 + cz * zeta) / 8.0
                    grad_y = 2.0 * cy * (1 + cx * xi) * (1 + cz * zeta) / 8.0
                    grad_z = 2.0 * cz * (1 + cx * xi) * (1 + cy * eta) / 8.0
                    strain[0, 3 * q] = grad_x
                    strain[1, 3 * q + 1] = grad_y
                    strain[2, 3 * q + 2] = grad_z
                    strain[3, 3 * q] = grad_y
                    strain[3, 3 * q + 1] = grad_x
                    strain[4, 3 * q + 1] = grad_z
                    strain[4, 3 * q + 2] = grad_y
                    strain[5, 3 * q] = grad_z
                    strain[5, 3 * q + 2] = grad_x
                    for c in range(3):
                        shape_rows[c, 3 * q + c] = value
                stiffness += strain.T @ elastic @ strain / 8.0
                mass_table += shape_rows.T @ shape_rows / 8.0
    return (stiffness.astype(np.float32), mass_table.astype(np.float32))


def filter_taps(radius):
    reach = radius - 1
    tap_list = []
    for a in range(-reach, reach + 1):
        for b in range(-reach, reach + 1):
            for c in range(-reach, reach + 1):
                weight = radius - float(np.sqrt(a * a + b * b + c * c))
                if weight > 0:
                    tap_list.append((a, b, c, weight))
    return tap_list


def cone_sum(padded, tap_list, reach, size_x, size_y, size_z):
    total = jnp.zeros(padded.shape[:-3] + (size_x, size_y, size_z), jnp.float32)
    for a, b, c, weight in tap_list:
        total = (
            total
            + weight
            * padded[
                ...,
                reach + a : reach + a + size_x,
                reach + b : reach + b + size_y,
                reach + c : reach + c + size_z,
            ]
        )
    return total


def element_forms(node_slab, stiffness, mass_table, size_y, size_z):
    pieces = []
    for a in (0, 1):
        for b in (0, 1):
            for d in (0, 1):
                pieces.append(node_slab[:, a, b : b + size_y, d : d + size_z])
    stacked = jnp.stack(pieces, 0)
    count = node_slab.shape[0] // 3
    vectors = (
        stacked.reshape(8, count, 3, size_y * size_z)
        .transpose(1, 0, 2, 3)
        .reshape(count, 24, size_y * size_z)
    )
    stiff_vec = jnp.einsum("pq,mqe->mpe", stiffness, vectors, precision=lax.Precision.HIGHEST)
    mass_vec = jnp.einsum("pq,mqe->mpe", mass_table, vectors, precision=lax.Precision.HIGHEST)
    return jnp.stack([jnp.sum(vectors * stiff_vec, axis=1), jnp.sum(vectors * mass_vec, axis=1)], 0)


def inside_range(start, length, limit):
    coords = start + jnp.arange(length, dtype=jnp.int32)
    return ((coords >= 0) & (coords < limit)).astype(jnp.float32)


def local(density, modes):
    rows_x, rows_y, depth = density.shape
    reach = RADIUS - 1
    tap_list = filter_taps(RADIUS)
    stiff_np, mass_np = element_tables()
    stiffness = jnp.asarray(stiff_np, jnp.float32)
    mass_table = jnp.asarray(mass_np, jnp.float32)
    total_x = rows_x * lax.axis_size("gx")
    total_y = rows_y * lax.axis_size("gy")
    elements = float(total_x * total_y * depth)
    count = modes.shape[0] // 3
    depth_pad = ((reach, reach),)
    dens_pad = padded_2(density, (("gx", 0), ("gy", 1)), reach)
    dens_pad = jnp.pad(dens_pad, ((0, 0), (0, 0)) + depth_pad)
    inside_x = inside_range(lax.axis_index("gx") * rows_x - reach, rows_x + 2 * reach, total_x)
    inside_y = inside_range(lax.axis_index("gy") * rows_y - reach, rows_y + 2 * reach, total_y)
    inside_z = jnp.pad(jnp.ones((depth,), jnp.float32), depth_pad)
    inside = inside_x[:, None, None] * inside_y[None, :, None] * inside_z[None, None, :]
    weight_sum = cone_sum(inside, tap_list, reach, rows_x, rows_y, depth)
    filtered = cone_sum(dens_pad, tap_list, reach, rows_x, rows_y, depth) / weight_sum
    denom = jnp.tanh(BETA_SHARP * ETA_MID) + jnp.tanh(BETA_SHARP * (1.0 - ETA_MID))
    sharp = jnp.tanh(BETA_SHARP * (filtered - ETA_MID))
    projected = (jnp.tanh(BETA_SHARP * ETA_MID) + sharp) / denom
    slope = BETA_SHARP * (1.0 - sharp * sharp) / denom
    young = YOUNG_MIN + projected**PENALTY * (1.0 - YOUNG_MIN)
    young_slope = PENALTY * projected**2 * (1.0 - YOUNG_MIN)
    received = passed_along(modes[:, 0:1], "gx", -1)
    extended = jnp.concatenate([modes, received], 1)
    received_edge = passed_along(extended[:, :, 0:1], "gy", -1)
    extended = jnp.concatenate([extended, received_edge], 2)
    extended = jnp.pad(extended, ((0, 0), (0, 0), (0, 0), (0, 1)))

    def row_forms(index):
        node_slab = lax.dynamic_slice_in_dim(extended, index, 2, 1).astype(jnp.float32)
        return element_forms(node_slab, stiffness, mass_table, rows_y, depth)

    forms = lax.map(row_forms, jnp.arange(rows_x, dtype=jnp.int32))
    forms = forms.reshape(rows_x, 2, count, rows_y, depth).transpose(1, 2, 0, 3, 4)
    stiff_form, mass_form = (forms[0], forms[1])
    local_stiff = jnp.sum(young * stiff_form, axis=(1, 2, 3))
    local_mass = jnp.sum(projected * mass_form, axis=(1, 2, 3))
    plane_pad = ((0, 0), (0, 0), (0, 0)) + depth_pad
    stiff_norm, mass_norm = lax.psum((local_stiff, local_mass), ("gx", "gy"))
    eigen_value = stiff_norm / mass_norm
    gradient = (
        elements
        * slope
        * (young_slope * stiff_form - eigen_value[:, None, None, None] * mass_form)
        / mass_norm[:, None, None, None]
    )
    scaled = gradient / weight_sum
    padded = padded_2(shortened(scaled), (("gx", 1), ("gy", 2)), reach).astype(scaled.dtype)
    padded = jnp.pad(padded, plane_pad)
    sensitivity = cone_sum(padded, tap_list, reach, rows_x, rows_y, depth)
    return sensitivity


def solution(mesh):
    return jax.shard_map(
        local,
        mesh=mesh,
        in_specs=(P("gx", "gy", None), P(None, "gx", "gy", None)),
        out_specs=P(None, "gx", "gy", None),
        check_vma=False,
    )
```

profile of v0, /device:TPU:160, one launch (start us, length us, event | category | flops | bytes accessed | tf_op | source)
XLA Modules:
  0.0 228.7 jit_solution(13951991048761779869)
XLA Ops:
  0.9 3.6 %collective-permute-start.4 = (bf16[12,1,16,256]{3,2,1,0:T(8,128)(2,1)S(1)}, bf16[12,1,16,256]{3,2,1,0:T(8,128)(2,1)S(1)}, u32[]{:S(2)}, u32[]{:S(2)}) collective-permute-start(bf16[12,1,16,256]{3,2,1,0:T(8,128)(2,1)S(1)} %slice.1163), channel_id=1, source_target_pairs={{16,0},{32,16},{48,32},{64,48},{80,64},{96,80},{112,96},{128,112},... | collective-permute-start | bytes 294920 | tf_op jit(solution)/shard_map/ppermute | solution.py:36
  7.2 5.8 %collective-permute-start.1 = (f32[2,16,256]{2,1,0:T(8,128)S(1)}, f32[2,16,256]{2,1,0:T(8,128)S(1)}, u32[]{:S(2)}, u32[]{:S(2)}) collective-permute-start(f32[2,16,256]{2,1,0:T(8,128)S(1)} %get-tuple-element.90), channel_id=1, source_target_pairs={{16,0},{32,16},{48,32},{64,48},{80,64},{96,80},{112,96},{128,112},... | collective-permute-start | bytes 98312 | tf_op jit(solution)/shard_map/ppermute | solution.py:26
  14.6 2.8 %collective-permute-start.3 = (f32[8,2,256]{2,1,0:T(2,128)S(1)}, f32[8,2,256]{2,1,0:T(2,128)S(1)}, u32[]{:S(2)}, u32[]{:S(2)}) collective-permute-start(f32[8,2,256]{2,1,0:T(2,128)S(1)} %get-tuple-element.83), channel_id=1, source_target_pairs={{1,0},{2,1},{3,2},{4,3},{5,4},{6,5},{7,6},{8,7},{9,8},{10,9},{11,1... | collective-permute-start | bytes 49160 | tf_op jit(solution)/shard_map/ppermute | solution.py:26
  17.5 3.0 %collective-permute-start.2 = (f32[8,2,256]{2,1,0:T(2,128)S(1)}, f32[8,2,256]{2,1,0:T(2,128)S(1)}, u32[]{:S(2)}, u32[]{:S(2)}) collective-permute-start(f32[8,2,256]{2,1,0:T(2,128)S(1)} %get-tuple-element.82), channel_id=1, source_target_pairs={{0,1},{1,2},{2,3},{3,4},{4,5},{5,6},{6,7},{7,8},{8,9},{9,10},{10,1... | collective-permute-start | bytes 49160 | tf_op jit(solution)/shard_map/ppermute | solution.py:24
  21.5 4.6 %collective-permute-done.2 = f32[8,2,256]{2,1,0:T(2,128)S(1)} collective-permute-done((f32[8,2,256]{2,1,0:T(2,128)S(1)}, f32[8,2,256]{2,1,0:T(2,128)S(1)}, u32[]{:S(2)}, u32[]{:S(2)}) %collective-permute-start.2) | collective-permute-done | bytes 16416 | tf_op jit(solution)/shard_map/ppermute | solution.py:24
  26.3 2.5 %subtract_multiply_fusion = (f32[4,16,256]{2,1,0:T(8,128)S(1)}, f32[4,16,256]{2,1,0:T(8,128)S(1)}, f32[4,16,256]{2,1,0:T(8,128)S(1)}) fusion(f32[8,2,256]{2,1,0:T(2,128)S(1)} %collective-permute-done.3, f32[8,16,256]{2,1,0:T(8,128)S(1)} %get-tuple-element.95, f32[8,20,260]{2,1,0:T(8,128)S(1)} %select_maximum_fusion, ...), kind=kLoop, calls=%fused_computation.694 | loop fusion | flops 6291456 | bytes 11239424 | tf_op jit(solution)/shard_map/mul | solution.py:183
  31.6 3.5 %collective-permute-done.5 = bf16[12,5,1,256]{3,2,1,0:T(2,128)(2,1)S(1)} collective-permute-done((bf16[12,5,1,256]{3,2,1,0:T(2,128)(2,1)S(1)}, bf16[12,5,1,256]{3,2,1,0:T(2,128)(2,1)S(1)}, u32[]{:S(2)}, u32[]{:S(2)}) %collective-permute-start.5) | collective-permute-done | bytes 30752 | tf_op jit(solution)/shard_map/ppermute | solution.py:36
  35.2 62.4 %while.11 = (s32[]{:T(128)}, f32[4,2,4,4096]{3,2,1,0:T(4,128)}, s32[4]{0:T(128)S(1)}, bf16[12,5,17,257]{3,2,1,0:T(8,128)(2,1)S(1)}, s32[]{:T(128)}, /*index=5*/f...) while((s32[]{:T(128)}, f32[4,2,4,4096]{3,2,1,0:T(4,128)}, ...), condition=%wide.region_3.4_spmd.clone, body=%wide.region_0.3_spmd.sunk.clone.sunk | while | flops 228170144 | bytes 20950052 | solution.py:174
  40.1 2.4 %stack.69 = f32[8,4,3,4096]{3,0,2,1:T(8,128)S(1)} concatenate(f32[1,4,3,4096]{3,0,2,1:T(1,128)S(1)} %stack.61, f32[1,4,3,4096]{3,0,2,1:T(1,128)S(1)} %stack.62, f32[1,4,3,4096]{3,0,2,1:T(1,128)S(1)} %stack.63, f32[1,4,3,4096]{3,0,2,1:T(1,128)S(1)} %stack.64, f32[1,4,3,4096]{3,0,2,1:T(1,128)S(1)} %stack.65, f32[1,4,3,4096]{3,0,2,1:T(1,128)S(1)} %stack.66, ...), dimensions={0} | concatenate | bytes 3145728 | tf_op jit(solution)/shard_map/while/body/eval_jaxpr/stack | solution.py:121
  43.5 3.3 %fusion.410 = f32[4,4096]{1,0:T(4,128)S(1)} fusion(f32[24,24,1]{1,0,2:T(8,128)S(1)} %get-tuple-element.160, f32[4,24,4096]{2,0,1:T(4,128)S(1)} %bitcast.76), kind=kOutput, calls=%fused_computation.7.clone.1 | convolution fusion | flops 114016256 | bytes 1640704 | tf_op jit(solution)/shard_map/while/body/eval_jaxpr/pq,mqe->mpe/dot_general | solution.py:129
  46.8 3.3 %fusion.411 = f32[4,4096]{1,0:T(4,128)S(1)} fusion(f32[24,24,1]{1,0,2:T(8,128)S(1)} %get-tuple-element.163, f32[4,24,4096]{2,0,1:T(4,128)S(1)} %bitcast.77), kind=kOutput, calls=%fused_computation.6.clone.1 | convolution fusion | flops 114016256 | bytes 1640704 | tf_op jit(solution)/shard_map/while/body/eval_jaxpr/pq,mqe->mpe/dot_general | solution.py:128
  55.7 2.4 %stack.69 = f32[8,4,3,4096]{3,0,2,1:T(8,128)S(1)} concatenate(f32[1,4,3,4096]{3,0,2,1:T(1,128)S(1)} %stack.61, f32[1,4,3,4096]{3,0,2,1:T(1,128)S(1)} %stack.62, f32[1,4,3,4096]{3,0,2,1:T(1,128)S(1)} %stack.63, f32[1,4,3,4096]{3,0,2,1:T(1,128)S(1)} %stack.64, f32[1,4,3,4096]{3,0,2,1:T(1,128)S(1)} %stack.65, f32[1,4,3,4096]{3,0,2,1:T(1,128)S(1)} %stack.66, ...), dimensions={0} | concatenate | bytes 3145728 | tf_op jit(solution)/shard_map/while/body/eval_jaxpr/stack | solution.py:121
  59.1 3.3 %fusion.410 = f32[4,4096]{1,0:T(4,128)S(1)} fusion(f32[24,24,1]{1,0,2:T(8,128)S(1)} %get-tuple-element.160, f32[4,24,4096]{2,0,1:T(4,128)S(1)} %bitcast.76), kind=kOutput, calls=%fused_computation.7.clone.1 | convolution fusion | flops 114016256 | bytes 1640704 | tf_op jit(solution)/shard_map/while/body/eval_jaxpr/pq,mqe->mpe/dot_general | solution.py:129
  62.4 3.3 %fusion.411 = f32[4,4096]{1,0:T(4,128)S(1)} fusion(f32[24,24,1]{1,0,2:T(8,128)S(1)} %get-tuple-element.163, f32[4,24,4096]{2,0,1:T(4,128)S(1)} %bitcast.77), kind=kOutput, calls=%fused_computation.6.clone.1 | convolution fusion | flops 114016256 | bytes 1640704 | tf_op jit(solution)/shard_map/while/body/eval_jaxpr/pq,mqe->mpe/dot_general | solution.py:128
  74.7 3.3 %fusion.410 = f32[4,4096]{1,0:T(4,128)S(1)} fusion(f32[24,24,1]{1,0,2:T(8,128)S(1)} %get-tuple-element.160, f32[4,24,4096]{2,0,1:T(4,128)S(1)} %bitcast.76), kind=kOutput, calls=%fused_computation.7.clone.1 | convolution fusion | flops 114016256 | bytes 1640704 | tf_op jit(solution)/shard_map/while/body/eval_jaxpr/pq,mqe->mpe/dot_general | solution.py:129
  78.0 3.3 %fusion.411 = f32[4,4096]{1,0:T(4,128)S(1)} fusion(f32[24,24,1]{1,0,2:T(8,128)S(1)} %get-tuple-element.163, f32[4,24,4096]{2,0,1:T(4,128)S(1)} %bitcast.77), kind=kOutput, calls=%fused_computation.6.clone.1 | convolution fusion | flops 114016256 | bytes 1640704 | tf_op jit(solution)/shard_map/while/body/eval_jaxpr/pq,mqe->mpe/dot_general | solution.py:128
  90.3 3.3 %fusion.410 = f32[4,4096]{1,0:T(4,128)S(1)} fusion(f32[24,24,1]{1,0,2:T(8,128)S(1)} %get-tuple-element.160, f32[4,24,4096]{2,0,1:T(4,128)S(1)} %bitcast.76), kind=kOutput, calls=%fused_computation.7.clone.1 | convolution fusion | flops 114016256 | bytes 1640704 | tf_op jit(solution)/shard_map/while/body/eval_jaxpr/pq,mqe->mpe/dot_general | solution.py:129
  93.6 3.3 %fusion.411 = f32[4,4096]{1,0:T(4,128)S(1)} fusion(f32[24,24,1]{1,0,2:T(8,128)S(1)} %get-tuple-element.163, f32[4,24,4096]{2,0,1:T(4,128)S(1)} %bitcast.77), kind=kOutput, calls=%fused_computation.6.clone.1 | convolution fusion | flops 114016256 | bytes 1640704 | tf_op jit(solution)/shard_map/while/body/eval_jaxpr/pq,mqe->mpe/dot_general | solution.py:128
  99.3 99.9 %all-reduce.4 = (f32[4]{0:T(128)S(1)}, f32[4]{0:T(128)S(1)}) all-reduce(f32[4]{0:T(128)S(1)} %get-tuple-element.56, f32[4]{0:T(128)S(1)} %get-tuple-element.55), channel_id=1, replica_groups=mesh['gx'=32,'gy'=16] {'gx','gy'}, use_global_device_ids=true, to_apply=%region_7.8 | all-reduce | flops 8 | bytes 64 | tf_op jit(solution)/shard_map/psum | solution.py:180
  199.4 2.8 %collective-permute-start.7 = (bf16[4,2,16,256]{3,2,1,0:T(8,128)(2,1)S(1)}, bf16[4,2,16,256]{3,2,1,0:T(8,128)(2,1)S(1)}, u32[]{:S(2)}, u32[]{:S(2)}) collective-permute-start(bf16[4,2,16,256]{3,2,1,0:T(8,128)(2,1)S(1)} %get-tuple-element.81), channel_id=1, source_target_pairs={{16,0},{32,16},{48,32},{64,48},{80,64},{96,80},{112,96},{128,112},... | collective-permute-start | bytes 196616 | tf_op jit(solution)/shard_map/ppermute | solution.py:26
  204.3 5.6 %collective-permute-done.6 = bf16[4,2,16,256]{3,2,1,0:T(8,128)(2,1)S(1)} collective-permute-done((bf16[4,2,16,256]{3,2,1,0:T(8,128)(2,1)S(1)}, bf16[4,2,16,256]{3,2,1,0:T(8,128)(2,1)S(1)}, u32[]{:S(2)}, u32[]{:S(2)}) %collective-permute-start.6) | collective-permute-done | bytes 65568 | tf_op jit(solution)/shard_map/ppermute | solution.py:24
  210.0 4.2 %collective-permute-start.9 = (bf16[4,8,2,256]{3,2,1,0:T(2,128)(2,1)S(1)}, bf16[4,8,2,256]{3,2,1,0:T(2,128)(2,1)S(1)}, u32[]{:S(2)}, u32[]{:S(2)}) collective-permute-start(bf16[4,8,2,256]{3,2,1,0:T(2,128)(2,1)S(1)} %get-tuple-element.79), channel_id=1, source_target_pairs={{1,0},{2,1},{3,2},{4,3},{5,4},{6,5},{7,6},{8,7},{9,8},{10,9},{11,1... | collective-permute-start | bytes 98312 | tf_op jit(solution)/shard_map/ppermute | solution.py:26
  216.2 6.9 %collective-permute-done.8 = bf16[4,8,2,256]{3,2,1,0:T(2,128)(2,1)S(1)} collective-permute-done((bf16[4,8,2,256]{3,2,1,0:T(2,128)(2,1)S(1)}, bf16[4,8,2,256]{3,2,1,0:T(2,128)(2,1)S(1)}, u32[]{:S(2)}, u32[]{:S(2)}) %collective-permute-start.8) | collective-permute-done | bytes 32800 | tf_op jit(solution)/shard_map/ppermute | solution.py:24
  223.2 5.5 %fusion.163 = f32[4,4,16,256]{3,2,1,0:T(8,128)} fusion(f32[4,8,20,256]{3,2,1,0:T(8,128)S(1)} %maximum_convert_fusion), kind=kLoop, calls=%fused_computation.274 | loop fusion | flops 11730944 | bytes 7602176 | tf_op jit(solution)/shard_map/add | solution.py:103
  (120 shorter events, 37.6 us)
Async XLA Ops:
  0.0 26.3 %copy-start.2 = (f32[4,16,256]{2,1,0:T(8,128)S(1)}, f32[4,16,256]{2,1,0:T(8,128)}, u32[]{:S(2)}) copy-start(f32[4,16,256]{2,1,0:T(8,128)} %param.6) | copy-start | bytes 196612
  0.9 27.9 %collective-permute-start.4 = (bf16[12,1,16,256]{3,2,1,0:T(8,128)(2,1)S(1)}, bf16[12,1,16,256]{3,2,1,0:T(8,128)(2,1)S(1)}, u32[]{:S(2)}, u32[]{:S(2)}) collective-permute-start(bf16[12,1,16,256]{3,2,1,0:T(8,128)(2,1)S(1)} %slice.1163), channel_id=1, source_target_pairs={{16,0},{32,16},{48,32},{64,48},{80,64},{96,80},{112,96},{128,112},... | collective-permute-start | bytes 294920 | tf_op jit(solution)/shard_map/ppermute | solution.py:36
  5.3 8.0 %collective-permute-start = (f32[2,16,256]{2,1,0:T(8,128)S(1)}, f32[2,16,256]{2,1,0:T(8,128)S(1)}, u32[]{:S(2)}, u32[]{:S(2)}) collective-permute-start(f32[2,16,256]{2,1,0:T(8,128)S(1)} %get-tuple-element.91), channel_id=1, source_target_pairs={{0,16},{16,32},{32,48},{48,64},{64,80},{80,96},{96,112},{112,128},... | collective-permute-start | bytes 98312 | tf_op jit(solution)/shard_map/ppermute | solution.py:24
  7.2 7.3 %collective-permute-start.1 = (f32[2,16,256]{2,1,0:T(8,128)S(1)}, f32[2,16,256]{2,1,0:T(8,128)S(1)}, u32[]{:S(2)}, u32[]{:S(2)}) collective-permute-start(f32[2,16,256]{2,1,0:T(8,128)S(1)} %get-tuple-element.90), channel_id=1, source_target_pairs={{16,0},{32,16},{48,32},{64,48},{80,64},{96,80},{112,96},{128,112},... | collective-permute-start | bytes 98312 | tf_op jit(solution)/shard_map/ppermute | solution.py:26
  14.6 6.9 %collective-permute-start.3 = (f32[8,2,256]{2,1,0:T(2,128)S(1)}, f32[8,2,256]{2,1,0:T(2,128)S(1)}, u32[]{:S(2)}, u32[]{:S(2)}) collective-permute-start(f32[8,2,256]{2,1,0:T(2,128)S(1)} %get-tuple-element.83), channel_id=1, source_target_pairs={{1,0},{2,1},{3,2},{4,3},{5,4},{6,5},{7,6},{8,7},{9,8},{10,9},{11,1... | collective-permute-start | bytes 49160 | tf_op jit(solution)/shard_map/ppermute | solution.py:26
  17.5 8.6 %collective-permute-start.2 = (f32[8,2,256]{2,1,0:T(2,128)S(1)}, f32[8,2,256]{2,1,0:T(2,128)S(1)}, u32[]{:S(2)}, u32[]{:S(2)}) collective-permute-start(f32[8,2,256]{2,1,0:T(2,128)S(1)} %get-tuple-element.82), channel_id=1, source_target_pairs={{0,1},{1,2},{2,3},{3,4},{4,5},{5,6},{6,7},{7,8},{8,9},{9,10},{10,1... | collective-permute-start | bytes 49160 | tf_op jit(solution)/shard_map/ppermute | solution.py:24
  28.8 6.4 %copy-start.3 = (f32[24,24,1]{1,0,2:T(8,128)S(1)}, f32[24,24,1]{1,0,2:T(8,128)}, u32[]{:S(2)}) copy-start(f32[24,24,1]{1,0,2:T(8,128)} %constant.831) | copy-start | bytes 6916
  28.9 6.4 %copy-start.4 = (f32[24,24,1]{1,0,2:T(8,128)S(1)}, f32[24,24,1]{1,0,2:T(8,128)}, u32[]{:S(2)}) copy-start(f32[24,24,1]{1,0,2:T(8,128)} %constant.832) | copy-start | bytes 6916
  28.9 6.1 %collective-permute-start.5 = (bf16[12,5,1,256]{3,2,1,0:T(2,128)(2,1)S(1)}, bf16[12,5,1,256]{3,2,1,0:T(2,128)(2,1)S(1)}, u32[]{:S(2)}, u32[]{:S(2)}) collective-permute-start(bf16[12,5,1,256]{3,2,1,0:T(2,128)(2,1)S(1)} %slice.1491), channel_id=1, source_target_pairs={{1,0},{2,1},{3,2},{4,3},{5,4},{6,5},{7,6},{8,7},{9,8},{10,9},{11,1... | collective-permute-start | bytes 92168 | tf_op jit(solution)/shard_map/ppermute | solution.py:36
  35.2 2.8 %copy-start = (bf16[12,5,17,257]{3,2,1,0:T(8,128)(2,1)}, bf16[12,5,17,257]{3,2,1,0:T(8,128)(2,1)S(1)}, u32[]{:S(2)}) copy-start(bf16[12,5,17,257]{3,2,1,0:T(8,128)(2,1)S(1)} %get-tuple-element.158) | copy-start | bytes 1572844 | tf_op jit(solution)/shard_map/while
  43.5 7.3 %copy-start.1 = (bf16[12,5,17,257]{3,2,1,0:T(8,128)(2,1)S(1)}, bf16[12,5,17,257]{3,2,1,0:T(8,128)(2,1)}, u32[]{:S(2)}) copy-start(bf16[12,5,17,257]{3,2,1,0:T(8,128)(2,1)} %copy-done) | copy-start | bytes 1572844 | tf_op jit(solution)/shard_map/while
  50.8 2.8 %copy-start = (bf16[12,5,17,257]{3,2,1,0:T(8,128)(2,1)}, bf16[12,5,17,257]{3,2,1,0:T(8,128)(2,1)S(1)}, u32[]{:S(2)}) copy-start(bf16[12,5,17,257]{3,2,1,0:T(8,128)(2,1)S(1)} %get-tuple-element.158) | copy-start | bytes 1572844 | tf_op jit(solution)/shard_map/while
  59.1 7.3 %copy-start.1 = (bf16[12,5,17,257]{3,2,1,0:T(8,128)(2,1)S(1)}, bf16[12,5,17,257]{3,2,1,0:T(8,128)(2,1)}, u32[]{:S(2)}) copy-start(bf16[12,5,17,257]{3,2,1,0:T(8,128)(2,1)} %copy-done) | copy-start | bytes 1572844 | tf_op jit(solution)/shard_map/while
  66.4 2.8 %copy-start = (bf16[12,5,17,257]{3,2,1,0:T(8,128)(2,1)}, bf16[12,5,17,257]{3,2,1,0:T(8,128)(2,1)S(1)}, u32[]{:S(2)}) copy-start(bf16[12,5,17,257]{3,2,1,0:T(8,128)(2,1)S(1)} %get-tuple-element.158) | copy-start | bytes 1572844 | tf_op jit(solution)/shard_map/while
  74.7 7.3 %copy-start.1 = (bf16[12,5,17,257]{3,2,1,0:T(8,128)(2,1)S(1)}, bf16[12,5,17,257]{3,2,1,0:T(8,128)(2,1)}, u32[]{:S(2)}) copy-start(bf16[12,5,17,257]{3,2,1,0:T(8,128)(2,1)} %copy-done) | copy-start | bytes 1572844 | tf_op jit(solution)/shard_map/while
  82.0 2.8 %copy-start = (bf16[12,5,17,257]{3,2,1,0:T(8,128)(2,1)}, bf16[12,5,17,257]{3,2,1,0:T(8,128)(2,1)S(1)}, u32[]{:S(2)}) copy-start(bf16[12,5,17,257]{3,2,1,0:T(8,128)(2,1)S(1)} %get-tuple-element.158) | copy-start | bytes 1572844 | tf_op jit(solution)/shard_map/while
  90.3 7.3 %copy-start.1 = (bf16[12,5,17,257]{3,2,1,0:T(8,128)(2,1)S(1)}, bf16[12,5,17,257]{3,2,1,0:T(8,128)(2,1)}, u32[]{:S(2)}) copy-start(bf16[12,5,17,257]{3,2,1,0:T(8,128)(2,1)} %copy-done) | copy-start | bytes 1572844 | tf_op jit(solution)/shard_map/while
  97.6 1.5 copy-start.5
  97.6 1.5 copy-start.6
  97.6 101.6 %copy-start.7 = (f32[4,16,256]{2,1,0:T(8,128)S(1)}, f32[4,16,256]{2,1,0:T(8,128)}, u32[]{:S(2)}) copy-start(f32[4,16,256]{2,1,0:T(8,128)} %get-tuple-element.84) | copy-start | bytes 196612
  199.4 4.9 %collective-permute-start.7 = (bf16[4,2,16,256]{3,2,1,0:T(8,128)(2,1)S(1)}, bf16[4,2,16,256]{3,2,1,0:T(8,128)(2,1)S(1)}, u32[]{:S(2)}, u32[]{:S(2)}) collective-permute-start(bf16[4,2,16,256]{3,2,1,0:T(8,128)(2,1)S(1)} %get-tuple-element.81), channel_id=1, source_target_pairs={{16,0},{32,16},{48,32},{64,48},{80,64},{96,80},{112,96},{128,112},... | collective-permute-start | bytes 196616 | tf_op jit(solution)/shard_map/ppermute | solution.py:26
  202.2 7.7 %collective-permute-start.6 = (bf16[4,2,16,256]{3,2,1,0:T(8,128)(2,1)S(1)}, bf16[4,2,16,256]{3,2,1,0:T(8,128)(2,1)S(1)}, u32[]{:S(2)}, u32[]{:S(2)}) collective-permute-start(bf16[4,2,16,256]{3,2,1,0:T(8,128)(2,1)S(1)} %get-tuple-element.80), channel_id=1, source_target_pairs={{0,16},{16,32},{32,48},{48,64},{64,80},{80,96},{96,112},{112,128},... | collective-permute-start | bytes 196616 | tf_op jit(solution)/shard_map/ppermute | solution.py:24
  210.0 6.2 %collective-permute-start.9 = (bf16[4,8,2,256]{3,2,1,0:T(2,128)(2,1)S(1)}, bf16[4,8,2,256]{3,2,1,0:T(2,128)(2,1)S(1)}, u32[]{:S(2)}, u32[]{:S(2)}) collective-permute-start(bf16[4,8,2,256]{3,2,1,0:T(2,128)(2,1)S(1)} %get-tuple-element.79), channel_id=1, source_target_pairs={{1,0},{2,1},{3,2},{4,3},{5,4},{6,5},{7,6},{8,7},{9,8},{10,9},{11,1... | collective-permute-start | bytes 98312 | tf_op jit(solution)/shard_map/ppermute | solution.py:26
  214.2 8.8 %collective-permute-start.8 = (bf16[4,8,2,256]{3,2,1,0:T(2,128)(2,1)S(1)}, bf16[4,8,2,256]{3,2,1,0:T(2,128)(2,1)S(1)}, u32[]{:S(2)}, u32[]{:S(2)}) collective-permute-start(bf16[4,8,2,256]{3,2,1,0:T(2,128)(2,1)S(1)} %get-tuple-element.78), channel_id=1, source_target_pairs={{0,1},{1,2},{2,3},{3,4},{4,5},{5,6},{6,7},{7,8},{8,9},{9,10},{10,1... | collective-permute-start | bytes 98312 | tf_op jit(solution)/shard_map/ppermute | solution.py:24
where the time goes:
time: 229 us
  blocking collectives  99.9 us (44%)
  starting transfers between devices  30.1 us (13%)
  local copies, waits for them, and re-layouts  29.5 us (13%)
  matrix products  26.4 us (12%)
  waiting for transfers between devices  20.9 us (9%)
  other arithmetic  12.7 us (6%)
  loops' own time  8.75 us (4%)
    psum x1, blocking collectives, local(): stiff_norm, mass_norm = lax.psum((local_stiff, local_mass), ('gx', 'gy'))  99.9 us
    ppermute x4, waiting for transfers between devices, padded_2(): lax.ppermute(tail, axis, [(i, (i + 1) % count) for i in range(ends)])  17 us
    another operation x36, local copies, waits for them, and re-layouts, element_forms(): stacked = jnp.stack(pieces, 0)  16 us
    ppermute x4, starting transfers between devices, padded_2(): lax.ppermute(head, axis, [((i + 1) % count, i) for i in range(ends)])  15.7 us
    dot_general x4, matrix products, element_forms(): jnp.einsum('pq,mqe->mpe', stiffness, vectors, precision=lax.Precision.HIG...  13.2 us
    dot_general x4, matrix products, element_forms(): jnp.einsum('pq,mqe->mpe', mass_table, vectors, precision=lax.Precision.HI...  13.2 us
    ppermute x4, starting transfers between devices, padded_2(): lax.ppermute(tail, axis, [(i, (i + 1) % count) for i in range(ends)])  8.93 us
    another operation x1, loops' own time, local(): forms = lax.map(row_forms, jnp.arange(rows_x, dtype=jnp.int32))  8.75 us
  transfers between devices with their start and end apart: 10, of which 5 were waited for; matrix products, arithmetic and copies ran while one was open for 3% of the time, Pallas kernels for 0%

commit v1 on v0

v1 whole, which is shorter than its diff:
```python
import functools
import math

import jax
import jax.numpy as jnp
import numpy as np
from jax import lax
from jax.experimental import pallas as pl
from jax.experimental.pallas import tpu as pltpu
from jax.sharding import PartitionSpec as P

RADIUS = 3
BETA_SHARP = 16.0
ETA_MID = 0.5
YOUNG_MIN = 0.001
POISSON = 0.3
MESH = pl.DeviceIdType.MESH

NX, NY = 32, 16
X, Y, Z = 4, 16, 256
L = 128
MODES = 4
CH = 3 * MODES
ZROWS = 24
F32 = jnp.float32
BF16 = jnp.bfloat16

NEIGHBOURS = [(a, b) for a in (-1, 0, 1) for b in (-1, 0, 1) if (a, b) != (0, 0)]


def weight(n):
    return max(0.0, RADIUS - math.sqrt(n))


def position():
    gx, gy = lax.axis_index("gx"), lax.axis_index("gy")
    return gx, gy


def neighbour(gx, gy, a, b):
    return (lax.rem(gx + a + NX, NX), lax.rem(gy + b + NY, NY))


def far_first(offsets, sizes):
    hops = lambda o: sum(min(v, n - v) for v, n in zip(o, sizes))
    return sorted((o for o in offsets if any(o)), key=lambda o: -hops(o))


GROUP_A = far_first([(i, j) for i in range(8) for j in range(4)], (8, 4))
GROUP_B = far_first([(i, j) for i in range(4) for j in range(4)], (4, 4))


def member_a(gx, gy, o):
    i, low = gx // 4, lax.rem(gx, 4)
    high, j = gy // 4, lax.rem(gy, 4)
    return (lax.rem(i + o[0], 8) * 4 + low, high * 4 + lax.rem(j + o[1], 4))


def member_b(gx, gy, o):
    i, low = gx // 4, lax.rem(gx, 4)
    high, j = gy // 4, lax.rem(gy, 4)
    return (i * 4 + lax.rem(low + o[0], 4), lax.rem(high + o[1], 4) * 4 + j)


def fold_depth(g0, g1, g2, lane):
    lo, hi = g0
    for k, (p, q) in ((1, g1), (2, g2)):
        p_up, q_up = pltpu.roll(p, k, 1), pltpu.roll(q, k, 1)
        p_dn, q_dn = pltpu.roll(p, L - k, 1), pltpu.roll(q, L - k, 1)
        first, last = lane < k, lane >= L - k
        lo = lo + (jnp.where(first, 0.0, p_up) + jnp.where(last, q_dn, p_dn))
        hi = hi + (jnp.where(first, p_up, q_up) + jnp.where(last, 0.0, q_dn))
    return lo, hi


def plane_sums(f, x1, x2):
    s0 = f[2]
    s1 = x1[2] + (f[1] + f[3])
    s2 = x1[1] + x1[3]
    s4 = x2[2] + (f[0] + f[4])
    s5 = (x1[0] + x1[4]) + (x2[1] + x2[3])
    s8 = x2[0] + x2[4]
    sums = ((0, s0), (1, s1), (2, s2), (4, s4), (5, s5), (8, s8))
    out = []
    for c in (0, 1, 4):
        total = None
        for n, s in sums:
            w = weight(n + c)
            if w > 0:
                total = w * s if total is None else total + w * s
        out.append(total)
    return out


def filter_density(ext, x, g, lane):
    planes = []
    for h in (0, 1):
        rows = lambda a, b: ext[h, x + 2 + a, 8 + 8 * g + b : 16 + 8 * g + b, :]
        f = [rows(0, b) for b in range(-2, 3)]
        x1 = [rows(-1, b) + rows(1, b) for b in range(-2, 3)]
        x2 = [rows(-2, b) + rows(2, b) for b in range(-2, 3)]
        planes.append(plane_sums(f, x1, x2))
    g0, g1, g2 = zip(*planes)
    return fold_depth(g0, g1, g2, lane)


def energies(t):
    lame = POISSON / ((1.0 + POISSON) * (1.0 - 2.0 * POISSON))
    shear = 1.0 / (2.0 * (1.0 + POISSON))
    sq = lambda v: v * v
    u, v, w = t
    total = lambda terms: functools.reduce(lambda p, q: p + q, terms)
    rigid = total([sq(c[0][0][0]) for c in t])
    diag = sq(u[1][0][0]) + sq(v[0][1][0]) + sq(w[0][0][1])
    first = total([sq(u[0][1][0]), sq(u[0][0][1]), sq(v[1][0][0]), sq(v[0][0][1]), sq(w[1][0][0]), sq(w[0][1][0])])
    second = total([sq(u[1][1][0]), sq(u[1][0][1]), sq(v[1][1][0]), sq(v[0][1][1]), sq(w[1][0][1]), sq(w[0][1][1])])
    other = total([sq(u[0][1][1]), sq(v[1][0][1]), sq(w[1][1][0])])
    third = total([sq(c[1][1][1]) for c in t])
    mass = rigid * (1 / 64) + (diag + first) * (1 / 192) + (second + other) * (1 / 576) + third * (1 / 1728)
    div = sq(u[1][0][0] + v[0][1][0] + w[0][0][1])
    div1 = total([sq(v[1][1][0] + w[1][0][1]), sq(u[1][1][0] + w[0][1][1]), sq(u[1][0][1] + v[0][1][1])])
    slide = total([sq(u[0][1][0] + v[1][0][0]), sq(u[0][0][1] + w[1][0][0]), sq(v[0][0][1] + w[0][1][0])])
    slide1 = total([sq(u[0][1][1] + v[1][0][1]), sq(u[0][1][1] + w[1][1][0]), sq(v[1][0][1] + w[1][1][0])])
    stiff = (
        (lame / 16) * div
        + (lame / 48) * div1
        + (shear / 8) * diag
        + (shear / 16) * slide
        + (shear / 48) * slide1
        + (shear / 16) * second
        + ((lame + 4 * shear) / 144) * third
    )
    return stiff, mass


def across(low, high):
    return [
        [
            [[low[c][j][k] + high[c][j][k] for k in (0, 1)] for j in (0, 1)],
            [[high[c][j][k] - low[c][j][k] for k in (0, 1)] for j in (0, 1)],
        ]
        for c in range(3)
    ]


def layer_of(zs, m, h, x, g):
    out = []
    for c in range(3):
        both = []
        for k in (0, 1):
            at = x * ZROWS + 8 * g
            here = zs[3 * m + c, 2 * k + h, at : at + 8, :]
            there = zs[3 * m + c, 2 * k + h, at + 1 : at + 9, :]
            both.append((here + there, there - here))
        out.append([[both[k][j] for k in (0, 1)] for j in (0, 1)])
    return out


def last_row_of(zs, yz, m, h, x):
    out = []
    for c in range(3):
        both = []
        for k in (0, 1):
            here = zs[3 * m + c, 2 * k + h, pl.ds(x * ZROWS + Y - 1, 8, stride=ZROWS), :]
            there = yz[2 * k + h, pl.ds(x * 16 + 3 * m + c, 8, stride=16), :]
            both.append((here + there, there - here))
        out.append([[both[k][j] for k in (0, 1)] for j in (0, 1)])
    return out


def kernel(
    dens_ref,
    modes_ref,
    out_ref,
    dext,
    wext,
    nodes,
    row0,
    first_row,
    next_row,
    zmat,
    zs,
    yz,
    forms,
    coef,
    ext,
    cone,
    slots_a,
    slots_b,
    in_sem,
    halo_send,
    halo_recv,
    field_send,
    field_recv,
    sum_send,
    sum_recv,
):
    gx, gy = position()
    lane = lax.broadcasted_iota(jnp.int32, (8, L), 1)

    loads = [
        pltpu.make_async_copy(dens_ref.at[:, :, L * h : L * (h + 1)], dext.at[h, 2:6, 8:24, :], in_sem.at[h])
        for h in (0, 1)
    ] + [pltpu.make_async_copy(modes_ref.at[:, x], nodes.at[x], in_sem.at[2 + x]) for x in range(X)]
    for load in loads:
        load.start()

    barrier = pltpu.get_barrier_semaphore()
    for a, b in NEIGHBOURS:
        pl.semaphore_signal(barrier, inc=1, device_id=neighbour(gx, gy, a, b), device_id_type=MESH)
    for o in GROUP_B:
        pl.semaphore_signal(barrier, inc=1, device_id=member_b(gx, gy, o), device_id_type=MESH)
    for o in GROUP_A:
        pl.semaphore_signal(barrier, inc=1, device_id=member_a(gx, gy, o), device_id_type=MESH)

    for load in loads:
        load.wait()

    def pack(c, _):
        for x in range(X):
            row0[pl.ds(x * 16 + c, 1), :] = nodes[x, c].astype(F32)[0:1, :]
        return 0

    lax.fori_loop(0, CH, pack, 0)
    first_row[...] = row0[...].astype(BF16)

    pl.semaphore_wait(barrier, len(NEIGHBOURS) + len(GROUP_A) + len(GROUP_B))

    def remote(src, dst, send, recv, a, b):
        return pltpu.make_async_remote_copy(
            src_ref=src,
            dst_ref=dst,
            send_sem=send,
            recv_sem=recv,
            device_id=neighbour(gx, gy, a, b),
            device_id_type=MESH,
        )

    src_x, dst_x = {-1: (2, 2), 0: (2, 4), 1: (4, 2)}, {-1: 6, 0: 2, 1: 0}
    halos = []
    far = sorted(NEIGHBOURS, key=lambda o: -abs(o[0]) - abs(o[1]))
    halos.append(remote(first_row.at[0:16], next_row.at[64:80], halo_send.at[8], halo_recv.at[8], -1, -1))
    for i, (a, b) in enumerate(far):
        x0, xn = src_x[a]
        y0, yn = {-1: (8, 8), 0: (8, 16), 1: (16, 8)}[b]
        y1 = {-1: 24, 0: 8, 1: 0}[b]
        halos.append(
            remote(
                dext.at[:, x0 : x0 + xn, y0 : y0 + yn, :],
                dext.at[:, dst_x[a] : dst_x[a] + xn, y1 : y1 + yn, :],
                halo_send.at[i],
                halo_recv.at[i],
                a,
                b,
            )
        )
    halos.append(remote(first_row, next_row.at[0:64], halo_send.at[9], halo_recv.at[9], 0, -1))
    halos.append(remote(nodes.at[0], nodes.at[4], halo_send.at[10], halo_recv.at[10], -1, 0))
    for halo in halos:
        halo.start()

    for h in (0, 1):
        for x in range(X + 4):
            ix = gx * X + (x - 2)
            inside_x = jnp.where((ix >= 0) & (ix < NX * X), 1.0, 0.0)
            iy = gy * Y - 8 + lax.broadcasted_iota(jnp.int32, (32, L), 0)
            wext[h, x] = jnp.where((iy >= 0) & (iy < NY * Y), inside_x, 0.0)

    def weights(x, _):
        for g in (0, 1):
            at = pl.ds(pl.multiple_of(x * Y + 8 * g, 8), 8)
            for h, s in enumerate(filter_density(wext, x, g, lane)):
                coef[0, h, at, :] = 1.0 / s
        return 0

    lax.fori_loop(0, X, weights, 0)

    row = lax.broadcasted_iota(jnp.int32, (Z, Z), 0)
    col = lax.broadcasted_iota(jnp.int32, (Z, Z), 1)
    here = jnp.where(row == col, 1.0, 0.0)
    there = jnp.where(row == col + 1, 1.0, 0.0)
    zmat[:, 0:Z] = (here + there).astype(BF16)
    zmat[:, Z : 2 * Z] = (there - here).astype(BF16)

    def depth(x, _):
        t = jnp.dot(nodes[x].reshape(CH * Y, Z), zmat[...], preferred_element_type=F32)
        at = pl.ds(pl.multiple_of(x * ZROWS, 8), Y)
        for c in range(CH):
            for q in range(4):
                zs[c, q, at, :] = t[c * Y : (c + 1) * Y, q * L : (q + 1) * L]
        return 0

    lax.fori_loop(0, X, depth, 0)

    def elements(x0, x1):
        def body(i, _):
            m, h = i // 2, lax.rem(i, 2)
            for g in (0, 1):
                low = layer_of(zs, m, h, x0, g)
                for x in range(x0, x1):
                    high = layer_of(zs, m, h, x + 1, g)
                    kq, mq = energies(across(low, high))
                    at = slice(x * Y + 8 * g, x * Y + 8 * g + 8)
                    forms[m, h, at, :] = kq
                    forms[MODES + m, h, at, :] = mq
                    low = high
            return 0

        lax.fori_loop(0, 2 * MODES, body, 0)

    elements(0, X - 1)

    for halo in halos:
        halo.wait_recv()

    @pl.when(gx == NX - 1)
    def _():
        nodes[4] = jnp.zeros((CH, Y, Z), BF16)
        next_row[64:80, :] = jnp.zeros((16, Z), BF16)
        dext[:, 6:8] = jnp.zeros((2, 2, 32, L), F32)

    @pl.when(gx == 0)
    def _():
        dext[:, 0:2] = jnp.zeros((2, 2, 32, L), F32)

    @pl.when(gy == NY - 1)
    def _():
        next_row[...] = jnp.zeros((80, Z), BF16)
        dext[:, :, 24:32] = jnp.zeros((2, 8, 8, L), F32)

    @pl.when(gy == 0)
    def _():
        dext[:, :, 0:8] = jnp.zeros((2, 8, 8, L), F32)

    depth(X, 0)
    t = jnp.dot(next_row[...], zmat[...], preferred_element_type=F32)
    for q in range(4):
        yz[q, 0:80, :] = t[:, q * L : (q + 1) * L]

    elements(X - 1, X)

    def last_row(i, _):
        m, h = i // 2, lax.rem(i, 2)
        kq, mq = energies(across(last_row_of(zs, yz, m, h, 0), last_row_of(zs, yz, m, h, 1)))
        forms[m, h, pl.ds(Y - 1, X, stride=Y), :] = kq[0:X]
        forms[MODES + m, h, pl.ds(Y - 1, X, stride=Y), :] = mq[0:X]
        return 0

    lax.fori_loop(0, 2 * MODES, last_row, 0)

    top = math.tanh(BETA_SHARP * ETA_MID)
    denom = top + math.tanh(BETA_SHARP * (1.0 - ETA_MID))

    def project(x, _):
        for g in (0, 1):
            at = pl.ds(pl.multiple_of(x * Y + 8 * g, 8), 8)
            for h, s in enumerate(filter_density(dext, x, g, lane)):
                share = coef[0, h, at, :]
                sharp = jnp.tanh(BETA_SHARP * (s * share - ETA_MID))
                projected = (top + sharp) * (1.0 / denom)
                slope = (BETA_SHARP / denom) * (1.0 - sharp * sharp) * share
                square = projected * projected
                coef[1, h, at, :] = YOUNG_MIN + square * projected * (1.0 - YOUNG_MIN)
                coef[2, h, at, :] = projected
                coef[3, h, at, :] = slope * (square * (3.0 * (1.0 - YOUNG_MIN)))
                coef[4, h, at, :] = slope
        return 0

    lax.fori_loop(0, X, project, 0)

    def scale(i, sums):
        h, x = i // X, lax.rem(i, X)
        sums = list(sums)
        for g in (0, 1):
            at = pl.ds(pl.multiple_of(x * Y + 8 * g, 8), 8)
            young, projected, a, b = (coef[n, h, at, :] for n in range(1, 5))
            for f in range(2 * MODES):
                q = forms[f, h, at, :]
                sums[f] = sums[f] + q * (young if f < MODES else projected)
                ext[h, x + 2, pl.ds((2 + 8 * g) * 8 + f, 8, stride=8), :] = q * (a if f < MODES else b)
        return tuple(sums)

    sums = lax.fori_loop(0, 2 * X, scale, tuple(jnp.zeros((8, L), F32) for _ in range(2 * MODES)))

    part = jnp.concatenate([jnp.sum(s, axis=0, keepdims=True) for s in sums], axis=0)
    for k in (64, 32, 16):
        part = part + pltpu.roll(part, k, 1)
    own = lane // 16 == lax.broadcasted_iota(jnp.int32, (8, L), 0)
    part = jnp.sum(jnp.where(own, part, 0.0), axis=0, keepdims=True)

    def group(slots, offsets, member, n, value):
        slots[0] = value
        for k, o in enumerate(offsets):
            pltpu.make_async_remote_copy(
                src_ref=slots.at[0],
                dst_ref=slots.at[k + 1],
                send_sem=sum_send.at[n],
                recv_sem=sum_recv.at[n],
                device_id=member(gx, gy, o),
                device_id_type=MESH,
            ).start()

    def group_wait(slots, sem):
        others = slots.at[pl.ds(1, slots.shape[0] - 1)]
        pltpu.make_async_copy(others, others, sem).wait()

    def group_sum(slots, n):
        group_wait(slots, sum_recv.at[n])
        return jnp.sum(slots[...], axis=0)

    group(slots_a, GROUP_A, member_a, 0, part)

    fields = []
    for i, (a, b) in enumerate(far):
        x0, xn = src_x[a]
        y0, yn = {-1: (2, 2), 0: (2, 16), 1: (16, 2)}[b]
        y1 = {-1: 18, 0: 2, 1: 0}[b]
        fields.append(
            remote(
                ext.at[:, x0 : x0 + xn, 8 * y0 : 8 * (y0 + yn), :],
                ext.at[:, dst_x[a] : dst_x[a] + xn, 8 * y1 : 8 * (y1 + yn), :],
                field_send.at[i],
                field_recv.at[i],
                a,
                b,
            )
        )
    for field in fields:
        field.start()

    group(slots_b, GROUP_B, member_b, 1, group_sum(slots_a, 0))

    for field in fields:
        field.wait_recv()

    @pl.when(gx == NX - 1)
    def _():
        ext[:, 6:8] = jnp.zeros((2, 2, 160, L), F32)

    @pl.when(gx == 0)
    def _():
        ext[:, 0:2] = jnp.zeros((2, 2, 160, L), F32)

    @pl.when(gy == NY - 1)
    def _():
        ext[:, :, 144:160] = jnp.zeros((2, 8, 16, L), F32)

    @pl.when(gy == 0)
    def _():
        ext[:, :, 0:16] = jnp.zeros((2, 8, 16, L), F32)

    def filter_fields(x, _):
        f, x1, x2 = [[], []], [[], []], [[], []]
        for y in range(Y + 4):
            for h in (0, 1):
                at = lambda a: ext[h, x + 2 + a, 8 * y : 8 * y + 8, :]
                f[h].append(at(0))
                x1[h].append(at(-1) + at(1))
                x2[h].append(at(-2) + at(2))
        for y in range(Y):
            planes = [plane_sums(f[h][y : y + 5], x1[h][y : y + 5], x2[h][y : y + 5]) for h in (0, 1)]
            g0, g1, g2 = zip(*planes)
            for h, s in enumerate(fold_depth(g0, g1, g2, lane)):
                cone[h, x, 8 * y : 8 * y + 8, :] = s
        return 0

    lax.fori_loop(0, X, filter_fields, 0)

    total = jnp.broadcast_to(group_sum(slots_b, 1), (8, L))
    total = jnp.sum(jnp.where(own, total, 0.0), axis=1, keepdims=True)
    elements_total = float(NX * X * NY * Y * Z)
    first, second = [], []
    for m in range(MODES):
        stiff_norm = jnp.broadcast_to(total[m : m + 1, :], (8, L))
        mass_norm = jnp.broadcast_to(total[MODES + m : MODES + m + 1, :], (8, L))
        first.append(elements_total / mass_norm)
        second.append(first[m] * (stiff_norm / mass_norm))

    def combine(x, _):
        for m in range(MODES):
            for g in (0, 1):
                for h in (0, 1):
                    stiff = cone[h, x, pl.ds(64 * g + m, 8, stride=8), :]
                    mass = cone[h, x, pl.ds(64 * g + MODES + m, 8, stride=8), :]
                    out_ref[m, x, 8 * g : 8 * g + 8, L * h : L * (h + 1)] = first[m] * stiff - second[m] * mass
        return 0

    lax.fori_loop(0, X, combine, 0)

    for copy in halos + fields:
        copy.wait_send()
    group_wait(slots_a, sum_send.at[0])
    group_wait(slots_b, sum_send.at[1])


def local(density, modes):
    return pl.pallas_call(
        kernel,
        out_shape=jax.ShapeDtypeStruct((MODES, X, Y, Z), F32),
        in_specs=[pl.BlockSpec(memory_space=pl.ANY)] * 2,
        out_specs=pl.BlockSpec(memory_space=pltpu.VMEM),
        scratch_shapes=[
            pltpu.VMEM((2, X + 4, 32, L), F32),
            pltpu.VMEM((2, X + 4, 32, L), F32),
            pltpu.VMEM((X + 1, CH, Y, Z), BF16),
            pltpu.VMEM((16 * X, Z), F32),
            pltpu.VMEM((16 * X, Z), BF16),
            pltpu.VMEM((16 * (X + 1), Z), BF16),
            pltpu.VMEM((Z, 2 * Z), BF16),
            pltpu.VMEM((CH, 4, 9 * ZROWS, L), F32),
            pltpu.VMEM((4, 9 * 16, L), F32),
            pltpu.VMEM((2 * MODES, 2, X * Y, L), F32),
            pltpu.VMEM((5, 2, X * Y, L), F32),
            pltpu.VMEM((2, X + 4, 8 * (Y + 4), L), F32),
            pltpu.VMEM((2, X, 8 * Y, L), F32),
            pltpu.VMEM((len(GROUP_A) + 1, 1, L), F32),
            pltpu.VMEM((len(GROUP_B) + 1, 1, L), F32),
            pltpu.SemaphoreType.DMA((2 + X,)),
            pltpu.SemaphoreType.DMA((11,)),
            pltpu.SemaphoreType.DMA((11,)),
            pltpu.SemaphoreType.DMA((8,)),
            pltpu.SemaphoreType.DMA((8,)),
            pltpu.SemaphoreType.DMA((2,)),
            pltpu.SemaphoreType.DMA((2,)),
        ],
        compiler_params=pltpu.CompilerParams(
            collective_id=0, has_side_effects=True, vmem_limit_bytes=40 * 1024 * 1024
        ),
    )(density, modes)


def solution(mesh):
    return jax.shard_map(
        local,
        mesh=mesh,
        in_specs=(P("gx", "gy", None), P(None, "gx", "gy", None)),
        out_specs=P(None, "gx", "gy", None),
        check_vma=False,
    )
```

time: 229 us -> 42.6 us (0.19)
  the two profiles are of different devices: /device:TPU:160 before, /device:TPU:6 now
where the time goes in v1:
time: 42.6 us; the launch traced here: 42.4 us
  Pallas kernels  39.8 us (93%)
  local copies, waits for them, and re-layouts  2.54 us (6%)
    pallas_call x1, Pallas kernels, local(): pl.pallas_call(kernel, out_shape=jax.ShapeDtypeStruct((MODES, X, Y, Z), F...  39.8 us
    unnamed x5, local copies, waits for them, and re-layouts  2.54 us

profile of v1, /device:TPU:6, one launch (start us, length us, event | category | flops | bytes accessed | tf_op | source)
XLA Modules:
  0.0 42.4 jit_solution(3473927862384311559)
XLA Ops:
  0.0 0.0 copy-start
  0.0 1.0 %copy-done = bf16[12,4,16,256]{3,2,1,0:T(8,128)(2,1)S(1)} copy-done((bf16[12,4,16,256]{3,2,1,0:T(8,128)(2,1)S(1)}, bf16[12,4,16,256]{3,2,1,0:T(8,128)(2,1)}, u32[]{:S(2)}) %copy-start) | copy-done | bytes 393240
  1.0 0.0 copy-start.1
  1.0 0.8 %copy-done.1 = f32[4,16,256]{2,1,0:T(8,128)S(1)} copy-done((f32[4,16,256]{2,1,0:T(8,128)S(1)}, f32[4,16,256]{2,1,0:T(8,128)}, u32[]{:S(2)}) %copy-start.1) | copy-done | bytes 65560
  1.8 39.8 %shard_map.28 = f32[4,4,16,256]{3,2,1,0:T(8,128)S(1)} custom-call(f32[4,16,256]{2,1,0:T(8,128)S(1)} %copy-done.1, bf16[12,4,16,256]{3,2,1,0:T(8,128)(2,1)S(1)} %copy-done), custom_call_target="tpu_custom_call" | custom-call | tf_op jit(solution)/shard_map/pallas_call | solution.py:497
  41.7 0.7 %copy.4 = f32[4,4,16,256]{3,2,1,0:T(8,128)} copy(f32[4,4,16,256]{3,2,1,0:T(8,128)S(1)} %shard_map.28) | data formatting | bytes 524288
Async XLA Ops:
  0.0 1.0 %copy-start = (bf16[12,4,16,256]{3,2,1,0:T(8,128)(2,1)S(1)}, bf16[12,4,16,256]{3,2,1,0:T(8,128)(2,1)}, u32[]{:S(2)}) copy-start(bf16[12,4,16,256]{3,2,1,0:T(8,128)(2,1)} %modes_ref.1) | copy-start | bytes 1179652
  1.0 0.8 %copy-start.1 = (f32[4,16,256]{2,1,0:T(8,128)S(1)}, f32[4,16,256]{2,1,0:T(8,128)}, u32[]{:S(2)}) copy-start(f32[4,16,256]{2,1,0:T(8,128)} %dens_ref.1) | copy-start | bytes 196612

commit v2 on v1

--- a/solution.py
+++ b/solution.py
@@ -184,6 +184,8 @@
     forms,
     coef,
     ext,
+    sent,
+    received,
     cone,
     slots_a,
     slots_b,
@@ -198,6 +200,9 @@
     gx, gy = position()
     lane = lax.broadcasted_iota(jnp.int32, (8, L), 1)
 
+    barrier = pltpu.get_barrier_semaphore()
+    for a, b in NEIGHBOURS:
+        pl.semaphore_signal(barrier, inc=1, device_id=neighbour(gx, gy, a, b), device_id_type=MESH)
     loads = [
         pltpu.make_async_copy(dens_ref.at[:, :, L * h : L * (h + 1)], dext.at[h, 2:6, 8:24, :], in_sem.at[h])
         for h in (0, 1)
@@ -205,9 +210,6 @@
     for load in loads:
         load.start()
 
-    barrier = pltpu.get_barrier_semaphore()
-    for a, b in NEIGHBOURS:
-        pl.semaphore_signal(barrier, inc=1, device_id=neighbour(gx, gy, a, b), device_id_type=MESH)
     for o in GROUP_B:
         pl.semaphore_signal(barrier, inc=1, device_id=member_b(gx, gy, o), device_id_type=MESH)
     for o in GROUP_A:
@@ -410,15 +412,21 @@
 
     group(slots_a, GROUP_A, member_a, 0, part)
 
+    def shorten(x, _):
+        for h in (0, 1):
+            sent[h, x] = ext[h, x + 2, 16:144, :].astype(BF16)
+        return 0
+
+    lax.fori_loop(0, X, shorten, 0)
     fields = []
     for i, (a, b) in enumerate(far):
         x0, xn = src_x[a]
-        y0, yn = {-1: (2, 2), 0: (2, 16), 1: (16, 2)}[b]
+        y0, yn = {-1: (0, 2), 0: (0, 16), 1: (14, 2)}[b]
         y1 = {-1: 18, 0: 2, 1: 0}[b]
         fields.append(
             remote(
-                ext.at[:, x0 : x0 + xn, 8 * y0 : 8 * (y0 + yn), :],
-                ext.at[:, dst_x[a] : dst_x[a] + xn, 8 * y1 : 8 * (y1 + yn), :],
+                sent.at[:, x0 - 2 : x0 - 2 + xn, 8 * y0 : 8 * (y0 + yn), :],
+                received.at[:, dst_x[a] : dst_x[a] + xn, 8 * y1 : 8 * (y1 + yn), :],
                 field_send.at[i],
                 field_recv.at[i],
                 a,
@@ -435,19 +443,27 @@
 
     @pl.when(gx == NX - 1)
     def _():
-        ext[:, 6:8] = jnp.zeros((2, 2, 160, L), F32)
+        received[:, 6:8] = jnp.zeros((2, 2, 160, L), BF16)
 
     @pl.when(gx == 0)
     def _():
-        ext[:, 0:2] = jnp.zeros((2, 2, 160, L), F32)
+        received[:, 0:2] = jnp.zeros((2, 2, 160, L), BF16)
 
     @pl.when(gy == NY - 1)
     def _():
-        ext[:, :, 144:160] = jnp.zeros((2, 8, 16, L), F32)
+        received[:, :, 144:160] = jnp.zeros((2, 8, 16, L), BF16)
 
     @pl.when(gy == 0)
     def _():
-        ext[:, :, 0:16] = jnp.zeros((2, 8, 16, L), F32)
+        received[:, :, 0:16] = jnp.zeros((2, 8, 16, L), BF16)
+
+    for h in (0, 1):
+        for x in range(X + 4):
+            if 2 <= x < X + 2:
+                for at in (slice(0, 16), slice(144, 160)):
+                    ext[h, x, at, :] = received[h, x, at, :].astype(F32)
+            else:
+                ext[h, x] = received[h, x].astype(F32)
 
     def filter_fields(x, _):
         f, x1, x2 = [[], []], [[], []], [[], []]
@@ -512,6 +528,8 @@
             pltpu.VMEM((2 * MODES, 2, X * Y, L), F32),
             pltpu.VMEM((5, 2, X * Y, L), F32),
             pltpu.VMEM((2, X + 4, 8 * (Y + 4), L), F32),
+            pltpu.VMEM((2, X, 8 * Y, L), BF16),
+            pltpu.VMEM((2, X + 4, 8 * (Y + 4), L), BF16),
             pltpu.VMEM((2, X, 8 * Y, L), F32),
             pltpu.VMEM((len(GROUP_A) + 1, 1, L), F32),
             pltpu.VMEM((len(GROUP_B) + 1, 1, L), F32),
@@ -526,7 +544,7 @@
         compiler_params=pltpu.CompilerParams(
             collective_id=0, has_side_effects=True, vmem_limit_bytes=40 * 1024 * 1024
         ),
-    )(density, modes)
+    )(*(pltpu.with_memory_space_constraint(a, pltpu.HBM) for a in (density, modes)))
 
 
 def solution(mesh):

time: 42.6 us -> 37.5 us (0.88)
  the two profiles are of different devices: /device:TPU:6 before, /device:TPU:1 now
where the time goes in v2:
time: 37.5 us; the launch traced here: 37.3 us
  Pallas kernels  36.6 us (98%)
  local copies, waits for them, and re-layouts  0.71 us (2%)
    pallas_call x1, Pallas kernels, local(): pl.pallas_call(kernel, out_shape=jax.ShapeDtypeStruct((MODES, X, Y, Z), F...  36.6 us

profile of v2, /device:TPU:1, one launch (start us, length us, event | category | flops | bytes accessed | tf_op | source)
XLA Modules:
  0.0 37.3 jit_solution(13043935437480626677)
XLA Ops:
  0.0 36.6 %shard_map.28 = f32[4,4,16,256]{3,2,1,0:T(8,128)S(1)} custom-call(f32[4,16,256]{2,1,0:T(8,128)} %dens_ref.1, bf16[12,4,16,256]{3,2,1,0:T(8,128)(2,1)} %modes_ref.1), custom_call_target="tpu_custom_call" | custom-call | tf_op jit(solution)/shard_map/pallas_call | solution.py:513
  36.6 0.7 %copy.4 = f32[4,4,16,256]{3,2,1,0:T(8,128)} copy(f32[4,4,16,256]{3,2,1,0:T(8,128)S(1)} %shard_map.28) | data formatting | bytes 524288

commit v3 on v2

--- a/solution.py
+++ b/solution.py
@@ -162,7 +162,7 @@
         both = []
         for k in (0, 1):
             here = zs[3 * m + c, 2 * k + h, pl.ds(x * ZROWS + Y - 1, 8, stride=ZROWS), :]
-            there = yz[2 * k + h, pl.ds(x * 16 + 3 * m + c, 8, stride=16), :]
+            there = yz[2 * k + h, pl.ds(x * CH + 3 * m + c, 8, stride=CH), :]
             both.append((here + there, there - here))
         out.append([[both[k][j] for k in (0, 1)] for j in (0, 1)])
     return out
@@ -175,6 +175,10 @@
     dext,
     wext,
     nodes,
+    side_out,
+    side_in,
+    corner_out,
+    corner_in,
     row0,
     first_row,
     next_row,
@@ -218,9 +222,20 @@
     for load in loads:
         load.wait()
 
+    corners = [(a, b) for a in (-1, 1) for b in (-1, 1)]
+    rows_from = {-1: slice(8, 10), 1: slice(22, 24)}
+    for h in (0, 1):
+        for s, b in enumerate((-1, 1)):
+            for x in range(X):
+                side_out[s, h, 2 * x : 2 * x + 2, :] = dext[h, x + 2, rows_from[b], :]
+        for k, (a, b) in enumerate(corners):
+            for i in (0, 1):
+                x = i if a == -1 else X - 2 + i
+                corner_out[k, 4 * h + 2 * i : 4 * h + 2 * i + 2, :] = dext[h, x + 2, rows_from[b], :]
+
     def pack(c, _):
         for x in range(X):
-            row0[pl.ds(x * 16 + c, 1), :] = nodes[x, c].astype(F32)[0:1, :]
+            row0[pl.ds(x * CH + c, 1), :] = nodes[x, c].astype(F32)[0:1, :]
         return 0
 
     lax.fori_loop(0, CH, pack, 0)
@@ -239,25 +254,16 @@
         )
 
     src_x, dst_x = {-1: (2, 2), 0: (2, 4), 1: (4, 2)}, {-1: 6, 0: 2, 1: 0}
-    halos = []
     far = sorted(NEIGHBOURS, key=lambda o: -abs(o[0]) - abs(o[1]))
-    halos.append(remote(first_row.at[0:16], next_row.at[64:80], halo_send.at[8], halo_recv.at[8], -1, -1))
-    for i, (a, b) in enumerate(far):
-        x0, xn = src_x[a]
-        y0, yn = {-1: (8, 8), 0: (8, 16), 1: (16, 8)}[b]
-        y1 = {-1: 24, 0: 8, 1: 0}[b]
-        halos.append(
-            remote(
-                dext.at[:, x0 : x0 + xn, y0 : y0 + yn, :],
-                dext.at[:, dst_x[a] : dst_x[a] + xn, y1 : y1 + yn, :],
-                halo_send.at[i],
-                halo_recv.at[i],
-                a,
-                b,
-            )
-        )
-    halos.append(remote(first_row, next_row.at[0:64], halo_send.at[9], halo_recv.at[9], 0, -1))
-    halos.append(remote(nodes.at[0], nodes.at[4], halo_send.at[10], halo_recv.at[10], -1, 0))
+    parts = [(first_row.at[0:16], next_row.at[CH * X : CH * X + 16], -1, -1)]
+    parts += [(corner_out.at[k], corner_in.at[k], a, b) for k, (a, b) in enumerate(corners)]
+    parts += [(side_out.at[s], side_in.at[s], 0, b) for s, b in enumerate((-1, 1))]
+    parts.append((first_row, next_row.at[0 : CH * X], 0, -1))
+    for a in (-1, 1):
+        x0 = src_x[a][0]
+        parts.append((dext.at[:, x0 : x0 + 2, 8:24, :], dext.at[:, dst_x[a] : dst_x[a] + 2, 8:24, :], a, 0))
+    parts.append((nodes.at[0], nodes.at[X], -1, 0))
+    halos = [remote(src, dst, halo_send.at[i], halo_recv.at[i], a, b) for i, (src, dst, a, b) in enumerate(parts)]
     for halo in halos:
         halo.start()
 
@@ -317,27 +323,42 @@
 
     @pl.when(gx == NX - 1)
     def _():
-        nodes[4] = jnp.zeros((CH, Y, Z), BF16)
-        next_row[64:80, :] = jnp.zeros((16, Z), BF16)
-        dext[:, 6:8] = jnp.zeros((2, 2, 32, L), F32)
+        nodes[X] = jnp.zeros((CH, Y, Z), BF16)
+        next_row[CH * X : CH * X + 16, :] = jnp.zeros((16, Z), BF16)
+        dext[:, 6:8, 8:24] = jnp.zeros((2, 2, Y, L), F32)
+        corner_in[0:2] = jnp.zeros((2, 8, L), F32)
 
     @pl.when(gx == 0)
     def _():
-        dext[:, 0:2] = jnp.zeros((2, 2, 32, L), F32)
+        dext[:, 0:2, 8:24] = jnp.zeros((2, 2, Y, L), F32)
+        corner_in[2:4] = jnp.zeros((2, 8, L), F32)
 
     @pl.when(gy == NY - 1)
     def _():
-        next_row[...] = jnp.zeros((80, Z), BF16)
-        dext[:, :, 24:32] = jnp.zeros((2, 8, 8, L), F32)
+        next_row[...] = jnp.zeros((CH * X + 16, Z), BF16)
+        side_in[0] = jnp.zeros((2, 8, L), F32)
+        corner_in[0] = jnp.zeros((8, L), F32)
+        corner_in[2] = jnp.zeros((8, L), F32)
 
     @pl.when(gy == 0)
     def _():
-        dext[:, :, 0:8] = jnp.zeros((2, 8, 8, L), F32)
+        side_in[1] = jnp.zeros((2, 8, L), F32)
+        corner_in[1] = jnp.zeros((8, L), F32)
+        corner_in[3] = jnp.zeros((8, L), F32)
+
+    rows_to = {-1: slice(24, 26), 1: slice(6, 8)}
+    for h in (0, 1):
+        for s, b in enumerate((-1, 1)):
+            for x in range(X):
+                dext[h, x + 2, rows_to[b], :] = side_in[s, h, 2 * x : 2 * x + 2, :]
+        for k, (a, b) in enumerate(corners):
+            for i in (0, 1):
+                dext[h, dst_x[a] + i, rows_to[b], :] = corner_in[k, 4 * h + 2 * i : 4 * h + 2 * i + 2, :]
 
     depth(X, 0)
     t = jnp.dot(next_row[...], zmat[...], preferred_element_type=F32)
     for q in range(4):
-        yz[q, 0:80, :] = t[:, q * L : (q + 1) * L]
+        yz[q, 0 : CH * X + 16, :] = t[:, q * L : (q + 1) * L]
 
     elements(X - 1, X)
 
@@ -519,12 +540,16 @@
             pltpu.VMEM((2, X + 4, 32, L), F32),
             pltpu.VMEM((2, X + 4, 32, L), F32),
             pltpu.VMEM((X + 1, CH, Y, Z), BF16),
-            pltpu.VMEM((16 * X, Z), F32),
-            pltpu.VMEM((16 * X, Z), BF16),
-            pltpu.VMEM((16 * (X + 1), Z), BF16),
+            pltpu.VMEM((2, 2, 8, L), F32),
+            pltpu.VMEM((2, 2, 8, L), F32),
+            pltpu.VMEM((4, 8, L), F32),
+            pltpu.VMEM((4, 8, L), F32),
+            pltpu.VMEM((CH * X, Z), F32),
+            pltpu.VMEM((CH * X, Z), BF16),
+            pltpu.VMEM((CH * X + 16, Z), BF16),
             pltpu.VMEM((Z, 2 * Z), BF16),
             pltpu.VMEM((CH, 4, 9 * ZROWS, L), F32),
-            pltpu.VMEM((4, 9 * 16, L), F32),
+            pltpu.VMEM((4, 112, L), F32),
             pltpu.VMEM((2 * MODES, 2, X * Y, L), F32),
             pltpu.VMEM((5, 2, X * Y, L), F32),
             pltpu.VMEM((2, X + 4, 8 * (Y + 4), L), F32),

time: 37.5 us -> 35.5 us (0.947)
  Pallas kernels: 36.6 us -> 34.7 us
    pallas_call x1, Pallas kernels: 36.6 us -> 34.7 us  [local(): pl.pallas_call(kernel, out_shape=jax.ShapeDtypeStruct((MODES, X, Y, Z), F...]
where the time goes in v3:
time: 35.5 us; the launch traced here: 35.4 us
  Pallas kernels  34.7 us (98%)
  local copies, waits for them, and re-layouts  0.71 us (2%)
    pallas_call x1, Pallas kernels, local(): pl.pallas_call(kernel, out_shape=jax.ShapeDtypeStruct((MODES, X, Y, Z), F...  34.7 us

profile of v3, /device:TPU:1, one launch (start us, length us, event | category | flops | bytes accessed | tf_op | source)
XLA Modules:
  0.0 35.4 jit_solution(16316811169631491604)
XLA Ops:
  0.0 34.7 %shard_map.28 = f32[4,4,16,256]{3,2,1,0:T(8,128)S(1)} custom-call(f32[4,16,256]{2,1,0:T(8,128)} %dens_ref.1, bf16[12,4,16,256]{3,2,1,0:T(8,128)(2,1)} %modes_ref.1), custom_call_target="tpu_custom_call" | custom-call | tf_op jit(solution)/shard_map/pallas_call | solution.py:534
  34.7 0.7 %copy.4 = f32[4,4,16,256]{3,2,1,0:T(8,128)} copy(f32[4,4,16,256]{3,2,1,0:T(8,128)S(1)} %shard_map.28) | data formatting | bytes 524288

commit v4 on v3

--- a/solution.py
+++ b/solution.py
@@ -37,29 +37,52 @@
     return gx, gy
 
 
+def exists(gx, gy, a, b):
+    inside = {-1: lambda i, n: [i > 0], 0: lambda i, n: [], 1: lambda i, n: [i < n - 1]}
+    return functools.reduce(jnp.logical_and, inside[a](gx, NX) + inside[b](gy, NY))
+
+
 def neighbour(gx, gy, a, b):
     return (lax.rem(gx + a + NX, NX), lax.rem(gy + b + NY, NY))
 
 
-def far_first(offsets, sizes):
-    hops = lambda o: sum(min(v, n - v) for v, n in zip(o, sizes))
-    return sorted((o for o in offsets if any(o)), key=lambda o: -hops(o))
-
-
-GROUP_A = far_first([(i, j) for i in range(8) for j in range(4)], (8, 4))
-GROUP_B = far_first([(i, j) for i in range(4) for j in range(4)], (4, 4))
+def ring(v, n):
+    v %= n
+    return min(v, n - v)
+
+
+def hops_a(o):
+    return ring(o[0], 8) + ring(o[1], 4)
+
+
+def hops_b(o):
+    return ring(o[0], 8)
+
+
+GROUP_A = sorted(((y, x) for y in range(8) for x in range(4) if (y, x) != (0, 0)), key=lambda o: -hops_a(o))
+GROUP_B = sorted(((z, c) for z in range(8) for c in range(2) if (z, c) != (0, 0)), key=lambda o: -hops_b(o))
+NEAR_A = [o for o in GROUP_A if hops_a(o) <= 3]
+NEAR_B = [o for o in GROUP_B if hops_b(o) <= 2]
+TOKENS_A = [(2, 1), (6, 1), (2, 3)]
+TOKENS_B = [(2, 0), (6, 0)]
+for group, near, tokens, hops, limit in (
+    (GROUP_A, NEAR_A, TOKENS_A, hops_a, 3),
+    (GROUP_B, NEAR_B, TOKENS_B, hops_b, 2),
+):
+    assert all(t in near for t in tokens)
+    assert all(o in near or any(hops((o[0] - t[0], o[1] - t[1])) <= limit for t in tokens) for o in group)
 
 
 def member_a(gx, gy, o):
-    i, low = gx // 4, lax.rem(gx, 4)
-    high, j = gy // 4, lax.rem(gy, 4)
-    return (lax.rem(i + o[0], 8) * 4 + low, high * 4 + lax.rem(j + o[1], 4))
+    y, low = gx // 4, lax.rem(gx, 4)
+    high, x = gy // 4, lax.rem(gy, 4)
+    return (lax.rem(y + o[0], 8) * 4 + low, high * 4 + lax.rem(x + o[1], 4))
 
 
 def member_b(gx, gy, o):
-    i, low = gx // 4, lax.rem(gx, 4)
-    high, j = gy // 4, lax.rem(gy, 4)
-    return (i * 4 + lax.rem(low + o[0], 4), lax.rem(high + o[1], 4) * 4 + j)
+    y, core = gx // 4, lax.rem(gx, 2)
+    z = lax.rem(2 * (gy // 4) + lax.rem(gx // 2, 2) + o[0], 8)
+    return (y * 4 + 2 * lax.rem(z, 2) + lax.rem(core + o[1], 2), (z // 2) * 4 + lax.rem(gy, 4))
 
 
 def fold_depth(g0, g1, g2, lane):
@@ -200,13 +223,18 @@
     field_recv,
     sum_send,
     sum_recv,
+    token,
 ):
     gx, gy = position()
     lane = lax.broadcasted_iota(jnp.int32, (8, L), 1)
 
     barrier = pltpu.get_barrier_semaphore()
     for a, b in NEIGHBOURS:
-        pl.semaphore_signal(barrier, inc=1, device_id=neighbour(gx, gy, a, b), device_id_type=MESH)
+
+        @pl.when(exists(gx, gy, a, b))
+        def _(a=a, b=b):
+            pl.semaphore_signal(barrier, inc=1, device_id=neighbour(gx, gy, a, b), device_id_type=MESH)
+
     loads = [
         pltpu.make_async_copy(dens_ref.at[:, :, L * h : L * (h + 1)], dext.at[h, 2:6, 8:24, :], in_sem.at[h])
         for h in (0, 1)
@@ -214,10 +242,10 @@
     for load in loads:
         load.start()
 
-    for o in GROUP_B:
+    for o in NEAR_A:
+        pl.semaphore_signal(barrier, inc=1, device_id=member_a(gx, gy, o), device_id_type=MESH)
+    for o in NEAR_B:
         pl.semaphore_signal(barrier, inc=1, device_id=member_b(gx, gy, o), device_id_type=MESH)
-    for o in GROUP_A:
-        pl.semaphore_signal(barrier, inc=1, device_id=member_a(gx, gy, o), device_id_type=MESH)
 
     for load in loads:
         load.wait()
@@ -233,16 +261,6 @@
                 x = i if a == -1 else X - 2 + i
                 corner_out[k, 4 * h + 2 * i : 4 * h + 2 * i + 2, :] = dext[h, x + 2, rows_from[b], :]
 
-    def pack(c, _):
-        for x in range(X):
-            row0[pl.ds(x * CH + c, 1), :] = nodes[x, c].astype(F32)[0:1, :]
-        return 0
-
-    lax.fori_loop(0, CH, pack, 0)
-    first_row[...] = row0[...].astype(BF16)
-
-    pl.semaphore_wait(barrier, len(NEIGHBOURS) + len(GROUP_A) + len(GROUP_B))
-
     def remote(src, dst, send, recv, a, b):
         return pltpu.make_async_remote_copy(
             src_ref=src,
@@ -254,7 +272,7 @@
         )
 
     src_x, dst_x = {-1: (2, 2), 0: (2, 4), 1: (4, 2)}, {-1: 6, 0: 2, 1: 0}
-    far = sorted(NEIGHBOURS, key=lambda o: -abs(o[0]) - abs(o[1]))
+    far = sorted(NEIGHBOURS, key=lambda o: (-abs(o[0]) - abs(o[1]), abs(o[0]), -o[0]))
     parts = [(first_row.at[0:16], next_row.at[CH * X : CH * X + 16], -1, -1)]
     parts += [(corner_out.at[k], corner_in.at[k], a, b) for k, (a, b) in enumerate(corners)]
     parts += [(side_out.at[s], side_in.at[s], 0, b) for s, b in enumerate((-1, 1))]
@@ -263,9 +281,64 @@
         x0 = src_x[a][0]
         parts.append((dext.at[:, x0 : x0 + 2, 8:24, :], dext.at[:, dst_x[a] : dst_x[a] + 2, 8:24, :], a, 0))
     parts.append((nodes.at[0], nodes.at[X], -1, 0))
-    halos = [remote(src, dst, halo_send.at[i], halo_recv.at[i], a, b) for i, (src, dst, a, b) in enumerate(parts)]
-    for halo in halos:
-        halo.start()
+    halos = [(remote(src, dst, halo_send.at[i], halo_recv.at[i], a, b), a, b) for i, (src, dst, a, b) in enumerate(parts)]
+    parts_f = []
+    for a, b in far:
+        x0, xn = src_x[a]
+        y0, yn = {-1: (0, 2), 0: (0, 16), 1: (14, 2)}[b]
+        y1 = {-1: 18, 0: 2, 1: 0}[b]
+        parts_f.append(
+            (
+                sent.at[:, x0 - 2 : x0 - 2 + xn, 8 * y0 : 8 * (y0 + yn), :],
+                received.at[:, dst_x[a] : dst_x[a] + xn, 8 * y1 : 8 * (y1 + yn), :],
+                a,
+                b,
+            )
+        )
+    fields = [
+        (remote(src, dst, field_send.at[i], field_recv.at[i], a, b), a, b) for i, (src, dst, a, b) in enumerate(parts_f)
+    ]
+
+    for _, dst, a, b in parts + parts_f:
+
+        @pl.when(jnp.logical_not(exists(gx, gy, -a, -b)))
+        def _(dst=dst):
+            dst[...] = jnp.zeros(dst.shape, dst.dtype)
+
+    def each(copies, step, sign):
+        for direction in far:
+            mine = [copy for copy, a, b in copies if (a, b) == direction]
+
+            @pl.when(exists(gx, gy, sign * direction[0], sign * direction[1]))
+            def _(mine=mine):
+                for copy in mine:
+                    step(copy)
+
+    def start(copies):
+        each(copies, lambda copy: copy.start(), 1)
+
+    def arrive(copies):
+        each(copies, lambda copy: copy.wait_recv(), -1)
+
+    def leave(copies):
+        each(copies, lambda copy: copy.wait_send(), 1)
+
+    def pack(c, _):
+        for x in range(X):
+            row0[pl.ds(x * CH + c, 1), :] = nodes[x, c].astype(F32)[0:1, :]
+        return 0
+
+    lax.fori_loop(0, CH, pack, 0)
+    first_row[...] = row0[...].astype(BF16)
+
+    along = lambda i, n: 1 + (i > 0).astype(jnp.int32) + (i < n - 1).astype(jnp.int32)
+    pl.semaphore_wait(barrier, along(gx, NX) * along(gy, NY) - 1 + len(NEAR_A) + len(NEAR_B))
+
+    start(halos)
+    for tokens, member in ((TOKENS_A, member_a), (TOKENS_B, member_b)):
+        for o in tokens:
+            back = (8 - o[0], (4 if member is member_a else 2) - o[1])
+            pl.semaphore_signal(token, inc=1, device_id=member(gx, gy, back), device_id_type=MESH)
 
     for h in (0, 1):
         for x in range(X + 4):
@@ -318,33 +391,7 @@
 
     elements(0, X - 1)
 
-    for halo in halos:
-        halo.wait_recv()
-
-    @pl.when(gx == NX - 1)
-    def _():
-        nodes[X] = jnp.zeros((CH, Y, Z), BF16)
-        next_row[CH * X : CH * X + 16, :] = jnp.zeros((16, Z), BF16)
-        dext[:, 6:8, 8:24] = jnp.zeros((2, 2, Y, L), F32)
-        corner_in[0:2] = jnp.zeros((2, 8, L), F32)
-
-    @pl.when(gx == 0)
-    def _():
-        dext[:, 0:2, 8:24] = jnp.zeros((2, 2, Y, L), F32)
-        corner_in[2:4] = jnp.zeros((2, 8, L), F32)
-
-    @pl.when(gy == NY - 1)
-    def _():
-        next_row[...] = jnp.zeros((CH * X + 16, Z), BF16)
-        side_in[0] = jnp.zeros((2, 8, L), F32)
-        corner_in[0] = jnp.zeros((8, L), F32)
-        corner_in[2] = jnp.zeros((8, L), F32)
-
-    @pl.when(gy == 0)
-    def _():
-        side_in[1] = jnp.zeros((2, 8, L), F32)
-        corner_in[1] = jnp.zeros((8, L), F32)
-        corner_in[3] = jnp.zeros((8, L), F32)
+    arrive(halos[1:7] + halos[8:10])
 
     rows_to = {-1: slice(24, 26), 1: slice(6, 8)}
     for h in (0, 1):
@@ -354,22 +401,6 @@
         for k, (a, b) in enumerate(corners):
             for i in (0, 1):
                 dext[h, dst_x[a] + i, rows_to[b], :] = corner_in[k, 4 * h + 2 * i : 4 * h + 2 * i + 2, :]
-
-    depth(X, 0)
-    t = jnp.dot(next_row[...], zmat[...], preferred_element_type=F32)
-    for q in range(4):
-        yz[q, 0 : CH * X + 16, :] = t[:, q * L : (q + 1) * L]
-
-    elements(X - 1, X)
-
-    def last_row(i, _):
-        m, h = i // 2, lax.rem(i, 2)
-        kq, mq = energies(across(last_row_of(zs, yz, m, h, 0), last_row_of(zs, yz, m, h, 1)))
-        forms[m, h, pl.ds(Y - 1, X, stride=Y), :] = kq[0:X]
-        forms[MODES + m, h, pl.ds(Y - 1, X, stride=Y), :] = mq[0:X]
-        return 0
-
-    lax.fori_loop(0, 2 * MODES, last_row, 0)
 
     top = math.tanh(BETA_SHARP * ETA_MID)
     denom = top + math.tanh(BETA_SHARP * (1.0 - ETA_MID))
@@ -391,25 +422,50 @@
 
     lax.fori_loop(0, X, project, 0)
 
-    def scale(i, sums):
+    arrive(halos[10:])
+    depth(X, 0)
+    elements(X - 1, X)
+
+    def scale(g, i, sums):
         h, x = i // X, lax.rem(i, X)
         sums = list(sums)
-        for g in (0, 1):
-            at = pl.ds(pl.multiple_of(x * Y + 8 * g, 8), 8)
-            young, projected, a, b = (coef[n, h, at, :] for n in range(1, 5))
-            for f in range(2 * MODES):
-                q = forms[f, h, at, :]
-                sums[f] = sums[f] + q * (young if f < MODES else projected)
-                ext[h, x + 2, pl.ds((2 + 8 * g) * 8 + f, 8, stride=8), :] = q * (a if f < MODES else b)
+        at = pl.ds(pl.multiple_of(x * Y + 8 * g, 8), 8)
+        young, projected, a, b = (coef[n, h, at, :] for n in range(1, 5))
+        for f in range(2 * MODES):
+            q = forms[f, h, at, :]
+            sums[f] = sums[f] + q * (young if f < MODES else projected)
+            ext[h, x + 2, pl.ds((2 + 8 * g) * 8 + f, 8, stride=8), :] = q * (a if f < MODES else b)
         return tuple(sums)
 
-    sums = lax.fori_loop(0, 2 * X, scale, tuple(jnp.zeros((8, L), F32) for _ in range(2 * MODES)))
-
-    part = jnp.concatenate([jnp.sum(s, axis=0, keepdims=True) for s in sums], axis=0)
+    zeros = tuple(jnp.zeros((8, L), F32) for _ in range(2 * MODES))
+    sums = lax.fori_loop(0, 2 * X, functools.partial(scale, 0), zeros)
+
+    arrive(halos[0:1] + halos[7:8])
+    t = jnp.dot(next_row[...], zmat[...], preferred_element_type=F32)
+    for q in range(4):
+        yz[q, 0 : CH * X + 16, :] = t[:, q * L : (q + 1) * L]
+
+    def last_row(i, _):
+        m, h = i // 2, lax.rem(i, 2)
+        kq, mq = energies(across(last_row_of(zs, yz, m, h, 0), last_row_of(zs, yz, m, h, 1)))
+        forms[m, h, pl.ds(Y - 1, X, stride=Y), :] = kq[0:X]
+        forms[MODES + m, h, pl.ds(Y - 1, X, stride=Y), :] = mq[0:X]
+        return 0
+
+    lax.fori_loop(0, 2 * MODES, last_row, 0)
+
+    sums = lax.fori_loop(0, 2 * X, functools.partial(scale, 1), sums)
+
+    part = list(sums)
     for k in (64, 32, 16):
-        part = part + pltpu.roll(part, k, 1)
+        half = len(part) // 2
+        upper = lane & k != 0
+        part = [
+            jnp.where(upper, q + pltpu.roll(q, k, 1), p + pltpu.roll(p, L - k, 1))
+            for p, q in zip(part[:half], part[half:])
+        ]
+    part = jnp.sum(part[0], axis=0, keepdims=True)
     own = lane // 16 == lax.broadcasted_iota(jnp.int32, (8, L), 0)
-    part = jnp.sum(jnp.where(own, part, 0.0), axis=0, keepdims=True)
 
     def group(slots, offsets, member, n, value):
         slots[0] = value
@@ -431,6 +487,7 @@
         group_wait(slots, sum_recv.at[n])
         return jnp.sum(slots[...], axis=0)
 
+    pl.semaphore_wait(token, len(TOKENS_A) + len(TOKENS_B))
     group(slots_a, GROUP_A, member_a, 0, part)
 
     def shorten(x, _):
@@ -439,44 +496,11 @@
         return 0
 
     lax.fori_loop(0, X, shorten, 0)
-    fields = []
-    for i, (a, b) in enumerate(far):
-        x0, xn = src_x[a]
-        y0, yn = {-1: (0, 2), 0: (0, 16), 1: (14, 2)}[b]
-        y1 = {-1: 18, 0: 2, 1: 0}[b]
-        fields.append(
-            remote(
-                sent.at[:, x0 - 2 : x0 - 2 + xn, 8 * y0 : 8 * (y0 + yn), :],
-                received.at[:, dst_x[a] : dst_x[a] + xn, 8 * y1 : 8 * (y1 + yn), :],
-                field_send.at[i],
-                field_recv.at[i],
-                a,
-                b,
-            )
-        )
-    for field in fields:
-        field.start()
+    start(fields)
 
     group(slots_b, GROUP_B, member_b, 1, group_sum(slots_a, 0))
 
-    for field in fields:
-        field.wait_recv()
-
-    @pl.when(gx == NX - 1)
-    def _():
-        received[:, 6:8] = jnp.zeros((2, 2, 160, L), BF16)
-
-    @pl.when(gx == 0)
-    def _():
-        received[:, 0:2] = jnp.zeros((2, 2, 160, L), BF16)
-
-    @pl.when(gy == NY - 1)
-    def _():
-        received[:, :, 144:160] = jnp.zeros((2, 8, 16, L), BF16)
-
-    @pl.when(gy == 0)
-    def _():
-        received[:, :, 0:16] = jnp.zeros((2, 8, 16, L), BF16)
+    arrive(fields)
 
     for h in (0, 1):
         for x in range(X + 4):
@@ -503,6 +527,9 @@
 
     lax.fori_loop(0, X, filter_fields, 0)
 
+    leave(halos + fields)
+    group_wait(slots_a, sum_send.at[0])
+    group_wait(slots_b, sum_send.at[1])
     total = jnp.broadcast_to(group_sum(slots_b, 1), (8, L))
     total = jnp.sum(jnp.where(own, total, 0.0), axis=1, keepdims=True)
     elements_total = float(NX * X * NY * Y * Z)
@@ -523,11 +550,6 @@
         return 0
 
     lax.fori_loop(0, X, combine, 0)
-
-    for copy in halos + fields:
-        copy.wait_send()
-    group_wait(slots_a, sum_send.at[0])
-    group_wait(slots_b, sum_send.at[1])
 
 
 def local(density, modes):
@@ -565,6 +587,7 @@
             pltpu.SemaphoreType.DMA((8,)),
             pltpu.SemaphoreType.DMA((2,)),
             pltpu.SemaphoreType.DMA((2,)),
+            pltpu.SemaphoreType.REGULAR,
         ],
         compiler_params=pltpu.CompilerParams(
             collective_id=0, has_side_effects=True, vmem_limit_bytes=40 * 1024 * 1024

time: 35.5 us -> 34.5 us (0.972)
  Pallas kernels: 34.7 us -> 33.6 us
    pallas_call x1, Pallas kernels: 34.7 us -> 33.6 us  [local(): pl.pallas_call(kernel, out_shape=jax.ShapeDtypeStruct((MODES, X, Y, Z), F...]
where the time goes in v4:
time: 34.5 us; the launch traced here: 34.3 us
  Pallas kernels  33.6 us (97%)
  local copies, waits for them, and re-layouts  0.71 us (2%)
    pallas_call x1, Pallas kernels, local(): pl.pallas_call(kernel, out_shape=jax.ShapeDtypeStruct((MODES, X, Y, Z), F...  33.6 us
    unnamed x1, local copies, waits for them, and re-layouts  0.71 us

profile of v4, /device:TPU:1, one launch (start us, length us, event | category | flops | bytes accessed | tf_op | source)
XLA Modules:
  0.0 34.3 jit_solution(14527884016469233244)
XLA Ops:
  0.0 33.6 %shard_map.28 = f32[4,4,16,256]{3,2,1,0:T(8,128)S(1)} custom-call(f32[4,16,256]{2,1,0:T(8,128)} %dens_ref.1, bf16[12,4,16,256]{3,2,1,0:T(8,128)(2,1)} %modes_ref.1), custom_call_target="tpu_custom_call" | custom-call | tf_op jit(solution)/shard_map/pallas_call | solution.py:556
  33.6 0.7 %copy.4 = f32[4,4,16,256]{3,2,1,0:T(8,128)} copy(f32[4,4,16,256]{3,2,1,0:T(8,128)S(1)} %shard_map.28) | data formatting | bytes 524288

commit v5 on v4

--- a/solution.py
+++ b/solution.py
@@ -308,6 +308,8 @@
     def each(copies, step, sign):
         for direction in far:
             mine = [copy for copy, a, b in copies if (a, b) == direction]
+            if not mine:
+                continue
 
             @pl.when(exists(gx, gy, sign * direction[0], sign * direction[1]))
             def _(mine=mine):
@@ -391,40 +393,41 @@
 
     elements(0, X - 1)
 
-    arrive(halos[1:7] + halos[8:10])
-
-    rows_to = {-1: slice(24, 26), 1: slice(6, 8)}
-    for h in (0, 1):
-        for s, b in enumerate((-1, 1)):
-            for x in range(X):
-                dext[h, x + 2, rows_to[b], :] = side_in[s, h, 2 * x : 2 * x + 2, :]
-        for k, (a, b) in enumerate(corners):
-            for i in (0, 1):
-                dext[h, dst_x[a] + i, rows_to[b], :] = corner_in[k, 4 * h + 2 * i : 4 * h + 2 * i + 2, :]
-
-    top = math.tanh(BETA_SHARP * ETA_MID)
-    denom = top + math.tanh(BETA_SHARP * (1.0 - ETA_MID))
-
-    def project(x, _):
-        for g in (0, 1):
-            at = pl.ds(pl.multiple_of(x * Y + 8 * g, 8), 8)
-            for h, s in enumerate(filter_density(dext, x, g, lane)):
-                share = coef[0, h, at, :]
-                sharp = jnp.tanh(BETA_SHARP * (s * share - ETA_MID))
-                projected = (top + sharp) * (1.0 / denom)
-                slope = (BETA_SHARP / denom) * (1.0 - sharp * sharp) * share
-                square = projected * projected
-                coef[1, h, at, :] = YOUNG_MIN + square * projected * (1.0 - YOUNG_MIN)
-                coef[2, h, at, :] = projected
-                coef[3, h, at, :] = slope * (square * (3.0 * (1.0 - YOUNG_MIN)))
-                coef[4, h, at, :] = slope
-        return 0
-
-    lax.fori_loop(0, X, project, 0)
-
     arrive(halos[10:])
     depth(X, 0)
     elements(X - 1, X)
+
+    def unpack(b):
+        s = (b + 1) // 2
+        to = {-1: slice(24, 26), 1: slice(6, 8)}[b]
+        for h in (0, 1):
+            for x in range(X):
+                dext[h, x + 2, to, :] = side_in[s, h, 2 * x : 2 * x + 2, :]
+            for k, (a, _) in enumerate(corners):
+                if k % 2 == s:
+                    for i in (0, 1):
+                        dext[h, dst_x[a] + i, to, :] = corner_in[k, 4 * h + 2 * i : 4 * h + 2 * i + 2, :]
+
+    top = math.tanh(BETA_SHARP * ETA_MID)
+    denom = top + math.tanh(BETA_SHARP * (1.0 - ETA_MID))
+
+    def project(g, x, _):
+        at = pl.ds(pl.multiple_of(x * Y + 8 * g, 8), 8)
+        for h, s in enumerate(filter_density(dext, x, g, lane)):
+            share = coef[0, h, at, :]
+            sharp = jnp.tanh(BETA_SHARP * (s * share - ETA_MID))
+            projected = (top + sharp) * (1.0 / denom)
+            slope = (BETA_SHARP / denom) * (1.0 - sharp * sharp) * share
+            square = projected * projected
+            coef[1, h, at, :] = YOUNG_MIN + square * projected * (1.0 - YOUNG_MIN)
+            coef[2, h, at, :] = projected
+            coef[3, h, at, :] = slope * (square * (3.0 * (1.0 - YOUNG_MIN)))
+            coef[4, h, at, :] = slope
+        return 0
+
+    arrive(halos[8:10] + halos[6:7] + halos[2:5:2])
+    unpack(1)
+    lax.fori_loop(0, X, functools.partial(project, 0), 0)
 
     def scale(g, i, sums):
         h, x = i // X, lax.rem(i, X)
@@ -439,6 +442,10 @@
 
     zeros = tuple(jnp.zeros((8, L), F32) for _ in range(2 * MODES))
     sums = lax.fori_loop(0, 2 * X, functools.partial(scale, 0), zeros)
+
+    arrive(halos[5:6] + halos[1:4:2])
+    unpack(-1)
+    lax.fori_loop(0, X, functools.partial(project, 1), 0)
 
     arrive(halos[0:1] + halos[7:8])
     t = jnp.dot(next_row[...], zmat[...], preferred_element_type=F32)

time: 34.5 us -> 33.6 us (0.974)
  Pallas kernels: 33.6 us -> 32.8 us
    pallas_call x1, Pallas kernels: 33.6 us -> 32.8 us  [local(): pl.pallas_call(kernel, out_shape=jax.ShapeDtypeStruct((MODES, X, Y, Z), F...]
where the time goes in v5:
time: 33.6 us; the launch traced here: 33.5 us
  Pallas kernels  32.8 us (98%)
  local copies, waits for them, and re-layouts  0.71 us (2%)
    pallas_call x1, Pallas kernels, local(): pl.pallas_call(kernel, out_shape=jax.ShapeDtypeStruct((MODES, X, Y, Z), F...  32.8 us
    unnamed x1, local copies, waits for them, and re-layouts  0.71 us

profile of v5, /device:TPU:1, one launch (start us, length us, event | category | flops | bytes accessed | tf_op | source)
XLA Modules:
  0.0 33.5 jit_solution(12514638660808073667)
XLA Ops:
  0.0 32.8 %shard_map.28 = f32[4,4,16,256]{3,2,1,0:T(8,128)S(1)} custom-call(f32[4,16,256]{2,1,0:T(8,128)} %dens_ref.1, bf16[12,4,16,256]{3,2,1,0:T(8,128)(2,1)} %modes_ref.1), custom_call_target="tpu_custom_call" | custom-call | tf_op jit(solution)/shard_map/pallas_call | solution.py:563
  32.8 0.7 %copy.4 = f32[4,4,16,256]{3,2,1,0:T(8,128)} copy(f32[4,4,16,256]{3,2,1,0:T(8,128)S(1)} %shard_map.28) | data formatting | bytes 524288

commit v6 on v5

--- a/solution.py
+++ b/solution.py
@@ -389,7 +389,7 @@
                     low = high
             return 0
 
-        lax.fori_loop(0, 2 * MODES, body, 0)
+        lax.fori_loop(0, 2 * MODES, body, 0, unroll=2 if x1 - x0 == 1 else 1)
 
     elements(0, X - 1)
 
@@ -411,8 +411,8 @@
     top = math.tanh(BETA_SHARP * ETA_MID)
     denom = top + math.tanh(BETA_SHARP * (1.0 - ETA_MID))
 
-    def project(g, x, _):
-        at = pl.ds(pl.multiple_of(x * Y + 8 * g, 8), 8)
+    def project(g, x):
+        at = slice(x * Y + 8 * g, x * Y + 8 * g + 8)
         for h, s in enumerate(filter_density(dext, x, g, lane)):
             share = coef[0, h, at, :]
             sharp = jnp.tanh(BETA_SHARP * (s * share - ETA_MID))
@@ -423,11 +423,11 @@
             coef[2, h, at, :] = projected
             coef[3, h, at, :] = slope * (square * (3.0 * (1.0 - YOUNG_MIN)))
             coef[4, h, at, :] = slope
-        return 0
 
     arrive(halos[8:10] + halos[6:7] + halos[2:5:2])
     unpack(1)
-    lax.fori_loop(0, X, functools.partial(project, 0), 0)
+    for x in range(X):
+        project(0, x)
 
     def scale(g, i, sums):
         h, x = i // X, lax.rem(i, X)
@@ -441,11 +441,12 @@
         return tuple(sums)
 
     zeros = tuple(jnp.zeros((8, L), F32) for _ in range(2 * MODES))
-    sums = lax.fori_loop(0, 2 * X, functools.partial(scale, 0), zeros)
+    sums = lax.fori_loop(0, 2 * X, functools.partial(scale, 0), zeros, unroll=2)
 
     arrive(halos[5:6] + halos[1:4:2])
     unpack(-1)
-    lax.fori_loop(0, X, functools.partial(project, 1), 0)
+    for x in range(X):
+        project(1, x)
 
     arrive(halos[0:1] + halos[7:8])
     t = jnp.dot(next_row[...], zmat[...], preferred_element_type=F32)
@@ -459,9 +460,9 @@
         forms[MODES + m, h, pl.ds(Y - 1, X, stride=Y), :] = mq[0:X]
         return 0
 
-    lax.fori_loop(0, 2 * MODES, last_row, 0)
-
-    sums = lax.fori_loop(0, 2 * X, functools.partial(scale, 1), sums)
+    lax.fori_loop(0, 2 * MODES, last_row, 0, unroll=4)
+
+    sums = lax.fori_loop(0, 2 * X, functools.partial(scale, 1), sums, unroll=2)
 
     part = list(sums)
     for k in (64, 32, 16):

time: 33.6 us -> 33.2 us (0.988)
  Pallas kernels: 32.8 us -> 32.3 us
    pallas_call x1, Pallas kernels: 32.8 us -> 32.3 us  [local(): pl.pallas_call(kernel, out_shape=jax.ShapeDtypeStruct((MODES, X, Y, Z), F...]
where the time goes in v6:
time: 33.2 us; the launch traced here: 33 us
  Pallas kernels  32.3 us (97%)
  local copies, waits for them, and re-layouts  0.71 us (2%)
    pallas_call x1, Pallas kernels, local(): pl.pallas_call(kernel, out_shape=jax.ShapeDtypeStruct((MODES, X, Y, Z), F...  32.3 us
    unnamed x1, local copies, waits for them, and re-layouts  0.71 us

profile of v6, /device:TPU:1, one launch (start us, length us, event | category | flops | bytes accessed | tf_op | source)
XLA Modules:
  0.0 33.0 jit_solution(12626407017274632173)
XLA Ops:
  0.0 32.3 %shard_map.28 = f32[4,4,16,256]{3,2,1,0:T(8,128)S(1)} custom-call(f32[4,16,256]{2,1,0:T(8,128)} %dens_ref.1, bf16[12,4,16,256]{3,2,1,0:T(8,128)(2,1)} %modes_ref.1), custom_call_target="tpu_custom_call" | custom-call | tf_op jit(solution)/shard_map/pallas_call | solution.py:564
  32.3 0.7 %copy.4 = f32[4,4,16,256]{3,2,1,0:T(8,128)} copy(f32[4,4,16,256]{3,2,1,0:T(8,128)S(1)} %shard_map.28) | data formatting | bytes 524288

commit v7 on v6

--- a/solution.py
+++ b/solution.py
@@ -59,30 +59,31 @@
     return ring(o[0], 8)
 
 
-GROUP_A = sorted(((y, x) for y in range(8) for x in range(4) if (y, x) != (0, 0)), key=lambda o: -hops_a(o))
-GROUP_B = sorted(((z, c) for z in range(8) for c in range(2) if (z, c) != (0, 0)), key=lambda o: -hops_b(o))
+GROUP_A = [(y, x, c) for y in range(8) for x in range(4) for c in range(2) if (y, x, c) != (0, 0, 0)]
+GROUP_A.sort(key=lambda o: -hops_a(o))
+GROUP_B = sorted(((z,) for z in range(1, 8)), key=lambda o: -hops_b(o))
 NEAR_A = [o for o in GROUP_A if hops_a(o) <= 3]
 NEAR_B = [o for o in GROUP_B if hops_b(o) <= 2]
-TOKENS_A = [(2, 1), (6, 1), (2, 3)]
-TOKENS_B = [(2, 0), (6, 0)]
+TOKENS_A = [(2, 1, 0), (6, 1, 0), (2, 3, 0)]
+TOKENS_B = [(2,), (6,)]
 for group, near, tokens, hops, limit in (
     (GROUP_A, NEAR_A, TOKENS_A, hops_a, 3),
     (GROUP_B, NEAR_B, TOKENS_B, hops_b, 2),
 ):
     assert all(t in near for t in tokens)
-    assert all(o in near or any(hops((o[0] - t[0], o[1] - t[1])) <= limit for t in tokens) for o in group)
+    assert all(o in near or any(hops([p - q for p, q in zip(o, t)]) <= limit for t in tokens) for o in group)
 
 
 def member_a(gx, gy, o):
-    y, low = gx // 4, lax.rem(gx, 4)
+    y, low, core = gx // 4, lax.rem(gx // 2, 2), lax.rem(gx, 2)
     high, x = gy // 4, lax.rem(gy, 4)
-    return (lax.rem(y + o[0], 8) * 4 + low, high * 4 + lax.rem(x + o[1], 4))
+    return (lax.rem(y + o[0], 8) * 4 + 2 * low + lax.rem(core + o[2], 2), high * 4 + lax.rem(x + o[1], 4))
 
 
 def member_b(gx, gy, o):
     y, core = gx // 4, lax.rem(gx, 2)
     z = lax.rem(2 * (gy // 4) + lax.rem(gx // 2, 2) + o[0], 8)
-    return (y * 4 + 2 * lax.rem(z, 2) + lax.rem(core + o[1], 2), (z // 2) * 4 + lax.rem(gy, 4))
+    return (y * 4 + 2 * lax.rem(z, 2) + core, (z // 2) * 4 + lax.rem(gy, 4))
 
 
 def fold_depth(g0, g1, g2, lane):
@@ -339,7 +340,7 @@
     start(halos)
     for tokens, member in ((TOKENS_A, member_a), (TOKENS_B, member_b)):
         for o in tokens:
-            back = (8 - o[0], (4 if member is member_a else 2) - o[1])
+            back = [n - v for n, v in zip((8, 4, 2), o)]
             pl.semaphore_signal(token, inc=1, device_id=member(gx, gy, back), device_id_type=MESH)
 
     for h in (0, 1):
@@ -449,9 +450,13 @@
         project(1, x)
 
     arrive(halos[0:1] + halos[7:8])
-    t = jnp.dot(next_row[...], zmat[...], preferred_element_type=F32)
-    for q in range(4):
-        yz[q, 0 : CH * X + 16, :] = t[:, q * L : (q + 1) * L]
+    after = next_row[...].astype(F32)
+    end = lax.broadcasted_iota(jnp.int32, (CH * X + 16, L), 1) == L - 1
+    moved = [pltpu.roll(after[:, h * L : (h + 1) * L], L - 1, 1) for h in (0, 1)]
+    moved = [jnp.where(end, moved[1], moved[0]), jnp.where(end, 0.0, moved[1])]
+    for h in (0, 1):
+        yz[h, 0 : CH * X + 16, :] = after[:, h * L : (h + 1) * L] + moved[h]
+        yz[2 + h, 0 : CH * X + 16, :] = moved[h] - after[:, h * L : (h + 1) * L]
 
     def last_row(i, _):
         m, h = i // 2, lax.rem(i, 2)
@@ -557,7 +562,7 @@
                     out_ref[m, x, 8 * g : 8 * g + 8, L * h : L * (h + 1)] = first[m] * stiff - second[m] * mass
         return 0
 
-    lax.fori_loop(0, X, combine, 0)
+    lax.fori_loop(0, X, combine, 0, unroll=2)
 
 
 def local(density, modes):

time: 33.2 us -> 32.8 us (0.988)
    pallas_call x1, Pallas kernels: 32.3 us -> 32 us  [local(): pl.pallas_call(kernel, out_shape=jax.ShapeDtypeStruct((MODES, X, Y, Z), F...]
where the time goes in v7:
time: 32.8 us; the launch traced here: 32.7 us
  Pallas kernels  32 us (98%)
  local copies, waits for them, and re-layouts  0.71 us (2%)
    pallas_call x1, Pallas kernels, local(): pl.pallas_call(kernel, out_shape=jax.ShapeDtypeStruct((MODES, X, Y, Z), F...  32 us
    unnamed x1, local copies, waits for them, and re-layouts  0.71 us

profile of v7, /device:TPU:1, one launch (start us, length us, event | category | flops | bytes accessed | tf_op | source)
XLA Modules:
  0.0 32.7 jit_solution(14934181342574186943)
XLA Ops:
  0.0 32.0 %shard_map.28 = f32[4,4,16,256]{3,2,1,0:T(8,128)S(1)} custom-call(f32[4,16,256]{2,1,0:T(8,128)} %dens_ref.1, bf16[12,4,16,256]{3,2,1,0:T(8,128)(2,1)} %modes_ref.1), custom_call_target="tpu_custom_call" | custom-call | tf_op jit(solution)/shard_map/pallas_call | solution.py:569
  32.0 0.7 %copy.4 = f32[4,4,16,256]{3,2,1,0:T(8,128)} copy(f32[4,4,16,256]{3,2,1,0:T(8,128)S(1)} %shard_map.28) | data formatting | bytes 524288

commit v8 on v7

--- a/solution.py
+++ b/solution.py
@@ -390,7 +390,7 @@
                     low = high
             return 0
 
-        lax.fori_loop(0, 2 * MODES, body, 0, unroll=2 if x1 - x0 == 1 else 1)
+        lax.fori_loop(0, 2 * MODES, body, 0, unroll=4 if x1 - x0 == 1 else 1)
 
     elements(0, X - 1)
 
@@ -442,7 +442,7 @@
         return tuple(sums)
 
     zeros = tuple(jnp.zeros((8, L), F32) for _ in range(2 * MODES))
-    sums = lax.fori_loop(0, 2 * X, functools.partial(scale, 0), zeros, unroll=2)
+    sums = lax.fori_loop(0, 2 * X, functools.partial(scale, 0), zeros, unroll=4)
 
     arrive(halos[5:6] + halos[1:4:2])
     unpack(-1)
@@ -465,9 +465,9 @@
         forms[MODES + m, h, pl.ds(Y - 1, X, stride=Y), :] = mq[0:X]
         return 0
 
-    lax.fori_loop(0, 2 * MODES, last_row, 0, unroll=4)
-
-    sums = lax.fori_loop(0, 2 * X, functools.partial(scale, 1), sums, unroll=2)
+    lax.fori_loop(0, 2 * MODES, last_row, 0, unroll=8)
+
+    sums = lax.fori_loop(0, 2 * X, functools.partial(scale, 1), sums, unroll=4)
 
     part = list(sums)
     for k in (64, 32, 16):
@@ -562,7 +562,7 @@
                     out_ref[m, x, 8 * g : 8 * g + 8, L * h : L * (h + 1)] = first[m] * stiff - second[m] * mass
         return 0
 
-    lax.fori_loop(0, X, combine, 0, unroll=2)
+    lax.fori_loop(0, X, combine, 0, unroll=4)
 
 
 def local(density, modes):

time: 32.8 us -> 32.7 us (level)
  no operation moved by 1% of the time
where the time goes in v8:
time: 32.7 us; the launch traced here: 32.6 us
  Pallas kernels  31.9 us (98%)
  local copies, waits for them, and re-layouts  0.71 us (2%)
    pallas_call x1, Pallas kernels, local(): pl.pallas_call(kernel, out_shape=jax.ShapeDtypeStruct((MODES, X, Y, Z), F...  31.9 us
    unnamed x1, local copies, waits for them, and re-layouts  0.71 us

profile of v8, /device:TPU:1, one launch (start us, length us, event | category | flops | bytes accessed | tf_op | source)
XLA Modules:
  0.0 32.6 jit_solution(15803666823103649346)
XLA Ops:
  0.0 31.9 %shard_map.28 = f32[4,4,16,256]{3,2,1,0:T(8,128)S(1)} custom-call(f32[4,16,256]{2,1,0:T(8,128)} %dens_ref.1, bf16[12,4,16,256]{3,2,1,0:T(8,128)(2,1)} %modes_ref.1), custom_call_target="tpu_custom_call" | custom-call | tf_op jit(solution)/shard_map/pallas_call | solution.py:569
  31.9 0.7 %copy.4 = f32[4,4,16,256]{3,2,1,0:T(8,128)} copy(f32[4,4,16,256]{3,2,1,0:T(8,128)S(1)} %shard_map.28) | data formatting | bytes 524288
